TPU v7x, 32 devices: a whole 2x2x4 slice. The times are simulated.
32 devices in a mesh: groups: 2 (over y), tok: 2 (over core), feat: 8 (over z, x).
Axes of the slice: x: 2, y: 2, z: 4, core: 2. Of those that a mesh axis runs over, the one named last changes fastest.
Arguments:
- inputs: bfloat16 [3, 512, 3584], P(None, ('groups', 'tok')), parts along dimension 1, may hold values from -6 to 6
- enc_weight: bfloat16 [3584, 16384], P('tok', 'feat'), may hold values from -0.09375 to 0.09375
- enc_bias: float32 [16384], P('feat'), may hold values from -0.6 to 0.2
- owner: int32 [536], P('feat'), may hold values from 0 to 528, as said below
Outputs:
- cooccurrence: bfloat16 [512, 1072, 512], P('tok', ('groups', 'feat')), parts along dimension 1
There are 2 independent parts, one for each index of `groups`. A program takes and returns all parts, laid end to end along the dimension named above; an argument that names none is the same for every part. Nothing has to cross between parts.
Inputs may be any that keep to these rules, and one draw needn't show every extreme that they name: `owner`: every tile number below 528 is held by exactly one slot; the value 528 marks an empty slot, and only the last of the 67 slots of one index of feat can be empty.
All inputs are finite; a program needn't handle non-finite values.
Results may differ from a plain program's by a relative error of at most 0.007.
Values may be sent and summed in bfloat16 or wider, within the bound.
No kernel may reach another device: no remote copies, remote signals or barrier semaphores. Data moves between devices by JAX's collectives and lax.ppermute only.
A program may use at most 448 MiB of HBM per device.

v0:
```python
import jax
import jax.numpy as jnp
import numpy as np
from jax import lax
from jax.sharding import PartitionSpec as P

F = 16384
TILE = 512


def tile_tables(block_count):
    row_list = []
    col_list = []
    for row_block in range(block_count):
        for col_block in range(row_block, block_count):
            row_list.append(row_block)
            col_list.append(col_block)
    row_list.append(0)
    col_list.append(0)
    return (np.array(row_list, np.int32), np.array(col_list, np.int32))


def block_ids(table, tile_total, row_table, col_table):
    matches = table[:, None] == jnp.arange(tile_total + 1, dtype=jnp.int32)[None, :]
    row_ids = jnp.sum(jnp.where(matches, jnp.asarray(row_table)[None, :], 0), axis=1).astype(
        jnp.int32
    )
    col_ids = jnp.sum(jnp.where(matches, jnp.asarray(col_table)[None, :], 0), axis=1).astype(
        jnp.int32
    )
    return (row_ids, col_ids)


def select_blocks(codes_batch, picker):
    block_count = picker.shape[1]
    blocks = codes_batch.reshape(
        codes_batch.shape[0], block_count, codes_batch.shape[1] // block_count
    )
    chosen = jnp.einsum("sn,knt->skt", picker, blocks, preferred_element_type=jnp.float32)
    return chosen.astype(jnp.bfloat16)


def body(inputs, enc_weight, enc_bias, owner):
    batches, tok_rows, model_width = inputs.shape
    flat_rows = inputs.reshape(batches * tok_rows, model_width)
    preact = jnp.dot(
        flat_rows,
        lax.all_gather(enc_weight, "tok", axis=0, tiled=True),
        preferred_element_type=jnp.float32,
    )
    code_rows = jnp.maximum(preact + enc_bias[None, :], 0.0).astype(jnp.bfloat16)
    block_count = F // TILE
    tile_total = block_count * (block_count + 1) // 2
    row_table, col_table = tile_tables(block_count)
    row_ids, col_ids = block_ids(owner, tile_total, row_table, col_table)
    slot_scale = (owner < tile_total).astype(jnp.float32) / (
        batches * tok_rows * lax.axis_size("tok")
    )
    block_range = jnp.arange(block_count, dtype=jnp.int32)
    row_picker = (row_ids[:, None] == block_range[None, :]).astype(jnp.bfloat16)
    col_picker = (col_ids[:, None] == block_range[None, :]).astype(jnp.bfloat16)
    gathered = [
        lax.all_gather(
            code_rows[batch_idx * tok_rows : (batch_idx + 1) * tok_rows], "feat", axis=1, tiled=True
        )
        for batch_idx in range(batches)
    ]
    row_sets = [select_blocks(codes_batch, row_picker) for codes_batch in gathered]
    col_sets = [select_blocks(codes_batch, col_picker) for codes_batch in gathered]

    def tile_terms(batch_idx):
        rows_blk = row_sets[batch_idx]
        product = jnp.einsum(
            "ska,skb->asb", rows_blk, col_sets[batch_idx], preferred_element_type=jnp.float32
        )
        return product * slot_scale[None, :, None]

    running = tile_terms(0)
    for batch_idx in range(1, batches):
        running = running + tile_terms(batch_idx)
    summed = lax.psum_scatter(running.astype(jnp.bfloat16), "tok", scatter_dimension=0, tiled=True)
    return summed


def solution(mesh):
    in_specs = (P(None, ("groups", "tok"), None), P("tok", "feat"), P("feat"), P("feat"))
    out_specs = P("tok", ("groups", "feat"), None)
    return jax.shard_map(body, mesh=mesh, in_specs=in_specs, out_specs=out_specs, check_vma=False)
```

profile of v0, /device:TPU:0, one launch (start us, length us, event | category | flops | bytes accessed | tf_op | source)
XLA Modules:
  0.0 536.2 jit_solution(5070475977529732305)
XLA Ops:
  6.5 0.7 all-gather.5.cloned.1.call-update
  7.3 0.0 all-gather.11.cloned.1.call-start
  7.3 31.4 %all-gather.5.cloned.1.call-done = bf16[3584,2048]{1,0:T(8,128)(2,1)} async-done(((bf16[1792,2048]{1,0:T(8,128)(2,1)}), bf16[3584,2048]{1,0:T(8,128)(2,1)}) %all-gather.5.cloned.1.call-update) | async-done | bytes 14680080 | tf_op jit(solution)/shard_map/all_gather | solution.py:48
  38.7 9.6 %maximum_convert_fusion = bf16[384,2048]{1,0:T(8,128)(2,1)S(1)} fusion(bf16[384,3584]{1,0:T(8,128)(2,1)S(1)} %bitcast.30, bf16[3584,2048]{1,0:T(8,128)(2,1)} %all-gather.5.cloned.1.call-done, f32[2048]{0:T(1024)} %param.8), kind=kOutput, calls=%fused_computation.10 | convolution fusion | flops 5639503872 | bytes 19013632 | tf_op jit(solution)/shard_map/dot_general | solution.py:46
  48.3 1.2 fusion.26
  49.5 0.0 all-gather.11.cloned.1.call-update
  49.6 0.0 all-gather.9.cloned.1.call-start
  49.6 0.7 all-gather.9.cloned.1.call-update
  50.3 0.0 all-gather.7.cloned.1.call-start
  50.3 0.5 all-gather.7.cloned.1.call-update
  50.9 0.0 reduce-scatter.2.cloned.1.call-start
  50.9 0.2 select_reduce_fusion.1
  51.2 73.1 %all-gather.11.cloned.1.call-done = bf16[128,16384]{1,0:T(8,128)(2,1)} async-done(((bf16[128,2048]{1,0:T(8,128)(2,1)}), bf16[128,16384]{1,0:T(8,128)(2,1)}) %all-gather.11.cloned.1.call-update) | async-done | bytes 4194320 | tf_op jit(solution)/shard_map/all_gather | solution.py:63
  124.2 5.9 %copy.17 = bf16[16,8,32,512]{3,2,1,0:T(8,128)(2,1)} copy(bf16[16,8,32,512]{3,1,2,0:T(8,128)(2,1)} %bitcast.37) | data formatting | bytes 8388608
  130.2 67.9 %all-gather.9.cloned.1.call-done = bf16[128,16384]{1,0:T(8,128)(2,1)} async-done(((bf16[128,2048]{1,0:T(8,128)(2,1)}), bf16[128,16384]{1,0:T(8,128)(2,1)}) %all-gather.9.cloned.1.call-update) | async-done | bytes 4194320 | tf_op jit(solution)/shard_map/all_gather | solution.py:63
  198.1 4.1 copy.16
  202.2 5.3 fusion.7
  207.6 5.1 fusion.14
  212.7 5.1 fusion.9
  217.7 5.1 fusion.16
  222.9 49.0 %all-gather.7.cloned.1.call-done = bf16[128,16384]{1,0:T(8,128)(2,1)} async-done(((bf16[128,2048]{1,0:T(8,128)(2,1)}), bf16[128,16384]{1,0:T(8,128)(2,1)}) %all-gather.7.cloned.1.call-update) | async-done | bytes 4194320 | tf_op jit(solution)/shard_map/all_gather | solution.py:63
  271.9 3.9 copy.15
  275.8 5.2 fusion.18
  281.0 5.1 fusion.11
  286.1 13.3 %copy.13 = bf16[67,128,512]{1,2,0:T(8,128)(2,1)} copy(bf16[67,128,512]{2,0,1:T(8,128)(2,1)} %fusion.7) | data formatting | bytes 17563648 | tf_op jit(solution)/shard_map/sn,knt->skt/dot_general | solution.py:39
  299.4 13.0 %copy.11 = bf16[67,128,512]{1,2,0:T(8,128)(2,1)} copy(bf16[67,128,512]{2,0,1:T(8,128)(2,1)} %fusion.9) | data formatting | bytes 17563648 | tf_op jit(solution)/shard_map/sn,knt->skt/dot_general | solution.py:39
  312.4 13.5 %copy.9 = bf16[67,128,512]{1,2,0:T(8,128)(2,1)} copy(bf16[67,128,512]{2,0,1:T(8,128)(2,1)} %fusion.11) | data formatting | bytes 17563648 | tf_op jit(solution)/shard_map/sn,knt->skt/dot_general | solution.py:39
  325.9 36.7 %fusion.1 = f32[67,512,512]{2,1,0:T(8,128)} fusion(bf16[67,128,512]{2,0,1:T(8,128)(2,1)} %fusion.18, bf16[67,128,512]{1,2,0:T(8,128)(2,1)} %copy.9), kind=kOutput, calls=%fused_computation.5 | convolution fusion | flops 4496293888 | bytes 87818240 | tf_op jit(solution)/shard_map/ska,skb->asb/dot_general | solution.py:73
  362.6 36.6 %fusion.2 = f32[67,512,512]{2,1,0:T(8,128)} fusion(bf16[67,128,512]{2,0,1:T(8,128)(2,1)} %fusion.16, bf16[67,128,512]{1,2,0:T(8,128)(2,1)} %copy.11), kind=kOutput, calls=%fused_computation.6 | convolution fusion | flops 4496293888 | bytes 87818240 | tf_op jit(solution)/shard_map/ska,skb->asb/dot_general | solution.py:73
  399.2 62.2 %fusion = bf16[512,67,512]{0,2,1:T(8,128)(2,1)} fusion(f32[67,512,512]{2,1,0:T(8,128)} %fusion.1, f32[67,512,512]{2,1,0:T(8,128)} %fusion.2, f32[67]{0:T(128)S(1)} %compare_select_fusion, bf16[67,128,512]{2,0,1:T(8,128)(2,1)} %fusion.14, bf16[67,128,512]{1,2,0:T(8,128)(2,1)} %copy.13), kind=kOutput, calls=%fused_computation.1 | convolution fusion | flops 4566548480 | bytes 193200400 | tf_op jit(solution)/shard_map/ska,skb->asb/dot_general | solution.py:73
  461.4 44.8 %reduce-scatter.2.cloned.1.call-done = bf16[256,67,512]{0,2,1:T(8,128)(2,1)} async-done(((bf16[512,67,512]{0,2,1:T(8,128)(2,1)}), bf16[256,67,512]{0,2,1:T(8,128)(2,1)}) %reduce-scatter.2.cloned.1.call-update) | async-done | bytes 17563664 | tf_op jit(solution)/shard_map/reduce_scatter | solution.py:81
  506.1 23.5 %copy.8 = bf16[256,67,512]{2,0,1:T(8,128)(2,1)} copy(bf16[256,67,512]{0,2,1:T(8,128)(2,1)} %reduce-scatter.2.cloned.1.call-done) | data formatting | bytes 35127296 | tf_op jit(solution)/shard_map/reduce_scatter | solution.py:81
  (15 shorter events, 0.0 us)
Async XLA Ops:
  6.5 32.2 %copy-start = (bf16[3,128,3584]{2,1,0:T(8,128)(2,1)S(1)}, bf16[3,128,3584]{2,1,0:T(8,128)(2,1)}, u32[]{:S(2)}) copy-start(bf16[3,128,3584]{2,1,0:T(8,128)(2,1)} %param.6) | copy-start | bytes 8257540
  6.5 32.1 %all-gather.5.cloned.1.call-start = ((), (), s32[]{:S(2)}) async-start(), calls=%async_computation.1 | async-start | bytes 22020096 | tf_op jit(solution)/shard_map/all_gather | solution.py:48
  7.3 117.0 %all-gather.11.cloned.1.call-start = ((), (), s32[]{:S(2)}) async-start(), calls=%async_computation.4 | async-start | bytes 4718592 | tf_op jit(solution)/shard_map/all_gather | solution.py:63
  38.7 12.2 %copy-start.3 = (s32[529]{0:T(1024)S(1)}, s32[529]{0:T(1024)}, u32[]{:S(2)}) copy-start(s32[529]{0:T(1024)} %constant.15.clone) | copy-start | bytes 6352
  38.7 12.2 %copy-start.4 = (s32[529]{0:T(1024)S(1)}, s32[529]{0:T(1024)}, u32[]{:S(2)}) copy-start(s32[529]{0:T(1024)} %constant.14.clone) | copy-start | bytes 6352
  38.7 12.2 %copy-start.5 = (s32[67]{0:T(128)S(1)}, s32[67]{0:T(128)}, u32[]{:S(2)}) copy-start(s32[67]{0:T(128)} %param.9) | copy-start | bytes 808
  49.6 148.6 %all-gather.9.cloned.1.call-start = ((), (), s32[]{:S(2)}) async-start(), calls=%async_computation.3 | async-start | bytes 4718592 | tf_op jit(solution)/shard_map/all_gather | solution.py:63
  50.3 221.6 %all-gather.7.cloned.1.call-start = ((), (), s32[]{:S(2)}) async-start(), calls=%async_computation.2 | async-start | bytes 4718592 | tf_op jit(solution)/shard_map/all_gather | solution.py:63
  50.9 455.3 %reduce-scatter.2.cloned.1.call-start = ((), (), s32[]{:S(2)}) async-start(), calls=%async_computation.5 | async-start | bytes 52690944 | tf_op jit(solution)/shard_map/reduce_scatter | solution.py:81
  198.1 4.1 copy-start.2
  461.4 68.3 %copy-start.1 = (bf16[3,128,3584]{2,1,0:T(8,128)(2,1)S(1)}, bf16[3,128,3584]{2,1,0:T(8,128)(2,1)}, u32[]{:S(2)}) copy-start(bf16[3,128,3584]{2,1,0:T(8,128)(2,1)} %param.6) | copy-start | bytes 8257540
Sparse Core Ops, SparseCore 0:
  8.9 29.7 all-gather.4
  49.7 74.5 all-gather.10
  126.4 71.6 all-gather.8
  200.2 71.6 all-gather.6
  461.5 44.5 reduce-scatter.1
where the time goes:
time: 538 us; the launch traced here: 536 us
  waiting for transfers between devices  268 us (50%)
  matrix products  176 us (33%)
  local copies, waits for them, and re-layouts  78.5 us (15%)
  between operations  13.2 us (2%)
    all_gather x3, waiting for transfers between devices, body(): lax.all_gather(code_rows[batch_idx * tok_rows:(batch_idx + 1) * tok_rows]...  190 us
    dot_general x3, matrix products, tile_terms(): jnp.einsum('ska,skb->asb', rows_blk, col_sets[batch_idx], preferred_eleme...  135 us
    reduce_scatter x1, waiting for transfers between devices, body(): lax.psum_scatter(running.astype(jnp.bfloat16), 'tok', scatter_dimension=0...  44.8 us
    dot_general x3, local copies, waits for them, and re-layouts, select_blocks(): jnp.einsum('sn,knt->skt', picker, blocks, preferred_element_type=jnp.floa...  39.8 us
    all_gather x1, waiting for transfers between devices, body(): lax.all_gather(enc_weight, 'tok', axis=0, tiled=True)  31.4 us
    dot_general x6, matrix products, select_blocks(): jnp.einsum('sn,knt->skt', picker, blocks, preferred_element_type=jnp.floa...  30.9 us
    reduce_scatter x1, local copies, waits for them, and re-layouts, body(): lax.psum_scatter(running.astype(jnp.bfloat16), 'tok', scatter_dimension=0...  23.5 us
    unnamed x15, local copies, waits for them, and re-layouts  13.9 us
  transfers between devices with their start and end apart: 5, of which 5 were waited for; matrix products, arithmetic and copies ran while one was open for 6% of the time, Pallas kernels for 0%

commit v1 on v0

v1 whole, which is shorter than its diff:
```python
import functools

import jax
import jax.numpy as jnp
import numpy as np
from jax import lax
from jax.experimental import pallas as pl
from jax.experimental.pallas import tpu as pltpu
from jax.sharding import PartitionSpec as P

F = 16384
TILE = 512


def tile_tables(block_count):
    row_list = []
    col_list = []
    for row_block in range(block_count):
        for col_block in range(row_block, block_count):
            row_list.append(row_block)
            col_list.append(col_block)
    row_list.append(0)
    col_list.append(0)
    return (np.array(row_list, np.int32), np.array(col_list, np.int32))


def block_ids(table, tile_total, row_table, col_table):
    matches = table[:, None] == jnp.arange(tile_total + 1, dtype=jnp.int32)[None, :]
    row_ids = jnp.sum(jnp.where(matches, jnp.asarray(row_table)[None, :], 0), axis=1).astype(
        jnp.int32
    )
    col_ids = jnp.sum(jnp.where(matches, jnp.asarray(col_table)[None, :], 0), axis=1).astype(
        jnp.int32
    )
    return (row_ids, col_ids)


def slot_tables(owner, tokens):
    block_count = F // TILE
    tile_total = block_count * (block_count + 1) // 2
    row_table, col_table = tile_tables(block_count)
    row_ids, col_ids = block_ids(owner, tile_total, row_table, col_table)
    slot_scale = (owner < tile_total).astype(jnp.float32) / tokens
    return row_ids, col_ids, slot_scale


def tiles_kernel(count, held, stage, where_ref, order_ref, bound_ref, row_ref, col_ref, scale_ref, *refs):
    pieces = refs[:count]
    out_ref, codes, done_ref, stop_buf, row_buf, col_buf, out_buf = refs[count + held : -3]
    in_sem, load_sem, out_sem = refs[-3:]
    depth, _, tokens, rows = row_buf.shape
    first = bound_ref[stage]
    last = bound_ref[stage + 1]
    my_row = lax.axis_index("tok") * rows

    arrivals = [
        pltpu.make_async_copy(piece, stop_buf.at[idx], in_sem.at[idx, 0])
        for idx, piece in enumerate(pieces)
    ]
    placed = [
        pltpu.make_async_copy(
            stop_buf.at[idx], codes.at[where_ref[idx // 2], idx % 2], in_sem.at[idx, 1]
        )
        for idx in range(count)
    ]
    for c in arrivals:
        c.start()
    for c, p in zip(arrivals, placed):
        c.wait()
        p.start()
    for p in placed:
        p.wait()

    def loads(t, buf):
        slot = order_ref[t]
        row_blk = row_ref[slot]
        col_blk = col_ref[slot]
        row_at = pl.multiple_of((row_blk & 1) * TILE + my_row, rows)
        col_at = pl.multiple_of((col_blk & 1) * TILE, TILE)
        return (
            pltpu.make_async_copy(
                codes.at[row_blk >> 1, :, :, pl.ds(row_at, rows)], row_buf.at[buf], load_sem.at[buf, 0]
            ),
            pltpu.make_async_copy(
                codes.at[col_blk >> 1, :, :, pl.ds(col_at, TILE)], col_buf.at[buf], load_sem.at[buf, 1]
            ),
        )

    def store(t, buf):
        return pltpu.make_async_copy(out_buf.at[buf], out_ref.at[order_ref[t]], out_sem.at[buf])

    def ahead(t):
        @pl.when(t < last)
        def _():
            for c in loads(t, lax.rem(t, depth)):
                c.start()

    for k in range(depth - 1):
        ahead(first + k)

    def one(t, carry):
        buf = lax.rem(t, depth)
        flip = lax.rem(t, 2)
        ahead(t + depth - 1)
        for c in loads(t, buf):
            c.wait()

        @pl.when(t - first >= 2)
        def _():
            store(t - 2, flip).wait()

        tile = lax.dot_general(
            row_buf[buf].reshape(2 * tokens, rows),
            col_buf[buf].reshape(2 * tokens, TILE),
            (((0,), (0,)), ((), ())),
            preferred_element_type=jnp.float32,
        )
        out_buf[flip] = (tile * scale_ref[order_ref[t]]).astype(out_buf.dtype)
        store(t, flip).start()
        return carry

    lax.fori_loop(first, last, one, 0)
    done_ref[0] = last
    for back in (2, 1):

        @pl.when(last - first >= back)
        def _():
            store(last - back, lax.rem(last - back, 2)).wait()


def tiles(stage, kept, state, shapes, where, tables):
    pieces = [piece for entry in kept for piece in entry[:2]]
    out, codes = shapes
    _, _, tokens, _ = codes.shape
    slots, rows, _ = out.shape
    depth = 6
    smem = pl.BlockSpec(memory_space=pltpu.SMEM)
    anywhere = pl.BlockSpec(memory_space=pl.ANY)
    lead = 1 + len(tables) + len(pieces)
    return pl.pallas_call(
        functools.partial(tiles_kernel, len(pieces), len(state), stage),
        out_shape=[out, codes, jax.ShapeDtypeStruct((1,), jnp.int32)],
        in_specs=[smem] * (1 + len(tables)) + [anywhere] * (len(pieces) + len(state)),
        out_specs=[anywhere, anywhere, smem],
        input_output_aliases={lead + k: k for k in range(len(state))},
        scratch_shapes=[
            pltpu.VMEM((len(pieces), *pieces[0].shape), codes.dtype),
            pltpu.VMEM((depth, 2, tokens, rows), codes.dtype),
            pltpu.VMEM((depth, 2, tokens, TILE), codes.dtype),
            pltpu.VMEM((2, rows, TILE), out.dtype),
            pltpu.SemaphoreType.DMA((len(pieces), 2)),
            pltpu.SemaphoreType.DMA((depth, 2)),
            pltpu.SemaphoreType.DMA((2,)),
        ],
        compiler_params=pltpu.CompilerParams(vmem_limit_bytes=56 * 1024 * 1024),
        cost_estimate=pl.CostEstimate(
            flops=slots * rows * TILE * 2 * tokens // 5,
            bytes_accessed=slots * (rows + TILE) * tokens // 5,
            transcendentals=0,
        ),
    )(where, *tables, *pieces, *state)


def stage_tables(row_ids, col_ids, half_stage):
    slots = row_ids.shape[0]
    width = half_stage.shape[0]
    pick = lambda ids: jnp.sum(
        jnp.where((ids >> 1)[:, None] == jnp.arange(width)[None, :], half_stage[None, :], 0), axis=1
    )
    stage = jnp.maximum(pick(row_ids), pick(col_ids))
    idx = jnp.arange(slots, dtype=jnp.int32)
    key = stage * slots + idx
    rank = jnp.sum((key[None, :] < key[:, None]).astype(jnp.int32), axis=1)
    order = jnp.sum(jnp.where(rank[None, :] == idx[:, None], idx[None, :], 0), axis=1)
    bounds = jnp.sum(
        (stage[None, :] < jnp.arange(8, dtype=jnp.int32)[:, None]).astype(jnp.int32), axis=1
    )
    return order.astype(jnp.int32), bounds.astype(jnp.int32)


def dev(z, x):
    return z * 2 + x


def z_pairs(moves):
    return [(dev(s, x), dev(d, x)) for s, d in moves for x in range(2)]


SWAP = [(0, 1), (1, 0)]
ACROSS = [(dev(z, x), dev(z, 1 - x)) for z in range(4) for x in range(2)]
NEXT = z_pairs([(0, 1), (1, 0), (2, 3), (3, 2)])
SECOND = z_pairs([(0, 2), (2, 0), (1, 3), (3, 1)])
MIDDLE = z_pairs([(1, 2), (2, 1)])
OUTWARD = z_pairs([(1, 0), (2, 3)])

STAGES = (
    ((0, 0, 0), (0, 0, 1), (0, 1, 0), (0, 1, 1), (1, 0, 0), (2, 0, 0)),
    ((1, 1, 0), (2, 1, 0), (2, 0, 1)),
    ((2, 1, 1), (3, 0, 0)),
    ((3, 1, 0), (3, 0, 1), (1, 0, 1)),
    ((3, 1, 1), (1, 1, 1)),
)


class Mover:
    def __init__(self):
        self.seen = ()
        self.pieces = {}

    def after(self, *arrays):
        self.seen = self.seen + arrays

    def send(self, array, pairs, axis="feat"):
        if self.seen:
            array = lax.optimization_barrier((array,) + self.seen)[0]
        return lax.ppermute(array, axis, pairs)

    def keep(self, key, array):
        self.pieces[key] = (array, self.send(array, SWAP, "tok"))
        return self.pieces[key][1]


def half_at(me, key):
    z, x, half = key
    return (me ^ (2 * z + x)) * 2 + half


def gather_and_tile(a, b, row_ids, col_ids, slot_scale):
    me = lax.axis_index("feat")
    half_index = jnp.arange(2 * lax.axis_size("feat"), dtype=jnp.int32)
    half_stage = sum(
        jnp.where(half_index == half_at(me, key), stage, 0)
        for stage, keys in enumerate(STAGES)
        for key in keys
    )
    order, bounds = stage_tables(row_ids, col_ids, half_stage)
    tables = (order, bounds, row_ids, col_ids, slot_scale)
    tokens, width = a.shape
    shapes = (
        jax.ShapeDtypeStruct((row_ids.shape[0], TILE // lax.axis_size("tok"), TILE), a.dtype),
        jax.ShapeDtypeStruct((half_index.shape[0], 2, tokens, width), a.dtype),
    )
    m = Mover()

    def work(stage, state):
        keys = STAGES[stage]
        where = jnp.stack([half_at(me, key) for key in keys]).astype(jnp.int32)
        kept = [m.pieces[key] for key in keys]
        *state, done = tiles(stage, kept, state, shapes, where, tables)
        m.after(done)
        return state

    x0a = m.send(a, ACROSS)
    n1a = m.send(a, NEXT)
    n2a = m.send(a, SECOND)
    x0b = m.send(b, ACROSS)
    m.keep((0, 0, 0), a)
    m.keep((0, 0, 1), b)

    m.after(x0a, x0b, n1a, n2a)
    x1a = m.send(n1a, ACROSS)
    x2a = m.send(n2a, ACROSS)
    n2b = m.send(b, SECOND)
    fa = m.send(n2a, OUTWARD)
    m.keep((0, 1, 0), x0a)
    m.keep((0, 1, 1), x0b)
    m.keep((1, 0, 0), n1a)
    m.keep((2, 0, 0), n2a)
    state = work(0, [])

    m.after(x1a, x2a, n2b, fa)
    x2b = m.send(n2b, ACROSS)
    ga = m.send(a, MIDDLE)
    fb = m.send(n2b, OUTWARD)
    m.keep((1, 1, 0), x1a)
    m.keep((2, 1, 0), x2a)
    m.keep((2, 0, 1), n2b)
    state = work(1, state)

    m.after(x2b, ga, fb)
    n3a = fa + ga
    x3a = m.send(n3a, ACROSS)
    gb = m.send(b, MIDDLE)
    n1b = m.send(b, NEXT)
    m.keep((2, 1, 1), x2b)
    m.keep((3, 0, 0), n3a)
    state = work(2, state)

    m.after(x3a, gb, n1b)
    n3b = fb + gb
    x3b = m.send(n3b, ACROSS)
    x1b = m.send(x0b, NEXT)
    m.keep((3, 1, 0), x3a)
    m.keep((3, 0, 1), n3b)
    m.keep((1, 0, 1), n1b)
    state = work(3, state)

    m.after(x3b, x1b)
    m.keep((3, 1, 1), x3b)
    m.keep((1, 1, 1), x1b)
    return work(4, state)[0]


def encode(inputs, enc_weight, enc_bias):
    batches, tok_rows, model_width = inputs.shape
    flat = inputs.reshape(batches * tok_rows, model_width)
    depth, features = enc_weight.shape
    first = lax.axis_index("tok") == 0
    lower, upper = flat[:, :depth], flat[:, depth:]
    theirs = jnp.where(first, upper, lower)
    other = lax.ppermute(theirs, "tok", SWAP)
    mine = jnp.where(first, lower, upper)
    halves = [slice(k * features // 2, (k + 1) * features // 2) for k in range(2)]
    near = [jnp.dot(mine, enc_weight[:, cols], preferred_element_type=jnp.float32) for cols in halves]
    other = lax.optimization_barrier((other, *near))[0]
    far = []
    for cols in halves:
        if far:
            other = lax.optimization_barrier((other, part))[0]
        part = jnp.dot(other, enc_weight[:, cols], preferred_element_type=jnp.float32)
        part = part.astype(jnp.bfloat16)
        far.append(lax.ppermute(part, "tok", SWAP))
    codes = []
    for k, cols in enumerate(halves):
        if codes:
            far[k] = lax.optimization_barrier((far[k], codes[-1]))[0]
        preact = near[k] + far[k].astype(jnp.float32)
        codes.append(jnp.maximum(preact + enc_bias[None, cols], 0.0).astype(jnp.bfloat16))
    return codes


def lines_body(inputs, enc_weight, enc_bias, owner):
    batches, tok_rows, _ = inputs.shape
    tables = slot_tables(owner, batches * tok_rows * lax.axis_size("tok"))
    a, b = encode(inputs, enc_weight, enc_bias)
    return gather_and_tile(a, b, *tables).transpose(1, 0, 2)


def select_blocks(codes_batch, picker):
    block_count = picker.shape[1]
    blocks = codes_batch.reshape(
        codes_batch.shape[0], block_count, codes_batch.shape[1] // block_count
    )
    chosen = jnp.einsum("sn,knt->skt", picker, blocks, preferred_element_type=jnp.float32)
    return chosen.astype(jnp.bfloat16)


def any_body(inputs, enc_weight, enc_bias, owner):
    batches, tok_rows, model_width = inputs.shape
    flat_rows = inputs.reshape(batches * tok_rows, model_width)
    preact = jnp.dot(
        flat_rows,
        lax.all_gather(enc_weight, "tok", axis=0, tiled=True),
        preferred_element_type=jnp.float32,
    )
    code_rows = jnp.maximum(preact + enc_bias[None, :], 0.0).astype(jnp.bfloat16)
    row_ids, col_ids, slot_scale = slot_tables(owner, batches * tok_rows * lax.axis_size("tok"))
    block_range = jnp.arange(F // TILE, dtype=jnp.int32)
    row_picker = (row_ids[:, None] == block_range[None, :]).astype(jnp.bfloat16)
    col_picker = (col_ids[:, None] == block_range[None, :]).astype(jnp.bfloat16)
    gathered = lax.all_gather(code_rows, "feat", axis=1, tiled=True)
    rows_blk = select_blocks(gathered, row_picker)
    cols_blk = select_blocks(gathered, col_picker)
    product = jnp.einsum("ska,skb->asb", rows_blk, cols_blk, preferred_element_type=jnp.float32)
    running = product * slot_scale[None, :, None]
    return lax.psum_scatter(running.astype(jnp.bfloat16), "tok", scatter_dimension=0, tiled=True)


def solution(mesh):
    in_specs = (P(None, ("groups", "tok"), None), P("tok", "feat"), P("feat"), P("feat"))
    out_specs = P("tok", ("groups", "feat"), None)
    lines = mesh.shape["feat"] == 8 and mesh.shape["tok"] == 2
    body = lines_body if lines else any_body
    return jax.shard_map(body, mesh=mesh, in_specs=in_specs, out_specs=out_specs, check_vma=False)
```

time: 538 us -> 191 us (0.36)
  waiting for transfers between devices: 268 us -> 62.9 us
  matrix products: 176 us -> 9.22 us
  Pallas kernels: 0 us -> 73.5 us
  local copies, waits for them, and re-layouts: 78.5 us -> 5.03 us
  starting transfers between devices: 0.16 us -> 30.7 us
  between operations: 13.2 us -> 0.5 us
  other arithmetic: 0.2 us -> 7.92 us
    all_gather x4 -> x0, waiting for transfers between devices: 221 us -> none  [the longest x3 190 us: body(): lax.all_gather(code_rows[batch_idx * tok_rows:(batch_idx + 1) * tok_rows]...]
    dot_general x10 -> x4, matrix products: 176 us -> 9.22 us  [the longest x2 6.05 us: encode(): jnp.dot(mine, enc_weight[:, cols], preferred_element_type=jnp.float32)]
    pallas_call x0 -> x5, Pallas kernels: none -> 73.5 us  [tiles(): pl.pallas_call(functools.partial(tiles_kernel, len(pieces), len(state), s...]
    ppermute x0 -> x35, waiting for transfers between devices: none -> 62.9 us  [the longest x32 61 us: send(): return lax.ppermute(array, axis, pairs)]
    reduce_scatter x1 -> x0, waiting for transfers between devices: 44.8 us -> none  [body(): lax.psum_scatter(running.astype(jnp.bfloat16), 'tok', scatter_dimension=0...]
    dot_general x3 -> x0, local copies, waits for them, and re-layouts: 39.8 us -> none  [select_blocks(): jnp.einsum('sn,knt->skt', picker, blocks, preferred_element_type=jnp.floa...]
    ppermute x0 -> x35, starting transfers between devices: none -> 30.7 us  [the longest x32 29.5 us: send(): return lax.ppermute(array, axis, pairs)]
    reduce_scatter x1 -> x0, local copies, waits for them, and re-layouts: 23.5 us -> none  [body(): lax.psum_scatter(running.astype(jnp.bfloat16), 'tok', scatter_dimension=0...]
  transfers between devices with their start and end apart: 5 -> 35, of which waited for: 5 -> 15; matrix products, arithmetic and copies ran while one was open for 6% -> 7% of each run, Pallas kernels for 0% -> 31%
where the time goes in v1:
time: 191 us; the launch traced here: 190 us
  Pallas kernels  73.5 us (38%)
  waiting for transfers between devices  62.9 us (33%)
  starting transfers between devices  30.7 us (16%)
  matrix products  9.22 us (5%)
  other arithmetic  7.92 us (4%)
  local copies, waits for them, and re-layouts  5.03 us (3%)
    pallas_call x5, Pallas kernels, tiles(): pl.pallas_call(functools.partial(tiles_kernel, len(pieces), len(state), s...  73.5 us
    ppermute x32, waiting for transfers between devices, send(): return lax.ppermute(array, axis, pairs)  61 us
    ppermute x32, starting transfers between devices, send(): return lax.ppermute(array, axis, pairs)  29.5 us
    dot_general x2, matrix products, encode(): jnp.dot(mine, enc_weight[:, cols], preferred_element_type=jnp.float32)  6.05 us
    unnamed x66, local copies, waits for them, and re-layouts  4.36 us
  transfers between devices with their start and end apart: 35, of which 15 were waited for; matrix products, arithmetic and copies ran while one was open for 7% of the time, Pallas kernels for 31%

profile of v1, /device:TPU:0, one launch (start us, length us, event | category | flops | bytes accessed | tf_op | source)
XLA Modules:
  0.0 189.7 jit_solution(6288660611754838762)
XLA Ops:
  0.0 2.0 %broadcast_select_fusion = bf16[384,1792]{1,0:T(8,128)(2,1)S(1)} fusion(pred[]{:T(512)S(6)} %eq.199, bf16[384,3584]{1,0:T(8,128)(2,1)} %bitcast.20), kind=kLoop, calls=%fused_computation.12 | loop fusion | flops 688128 | bytes 4128769 | tf_op jit(solution)/shard_map/jit(_where)/select_n | solution.py:310
  2.6 4.4 %fusion.2 = f32[384,1024]{1,0:T(8,128)S(1)} fusion(bf16[1792,2048]{1,0:T(8,128)(2,1)} %param.7, pred[]{:T(512)S(6)} %eq.199, bf16[384,3584]{1,0:T(8,128)(2,1)S(1)} %bitcast.21), kind=kOutput, calls=%fused_computation.2 | convolution fusion | flops 1409974272 | bytes 7995393 | tf_op jit(solution)/shard_map/dot_general | solution.py:314
  7.1 1.6 fusion.6
  8.7 1.6 fusion.11
  10.8 1.6 fusion.8
  13.1 1.7 collective-permute-done.1
  15.1 2.7 %collective-permute-start.4 = (bf16[384,1024]{1,0:T(8,128)(2,1)S(1)}, bf16[384,1024]{1,0:T(8,128)(2,1)S(1)}, u32[]{:S(2)}, u32[]{:S(2)}) collective-permute-start(bf16[384,1024]{1,0:T(8,128)(2,1)S(1)} %maximum_convert_fusion.refs_2_), channel_id=1, source_target_pairs={{0,1},{1,0},{2,3},{3,2},{4,5},{5,4},{6,7},{7,6},{8,9},{9,8},{10,11... | collective-permute-start | bytes 2359304 | tf_op jit(solution)/shard_map/ppermute | solution.py:216
  17.8 2.6 %collective-permute-start.6 = (bf16[384,1024]{1,0:T(8,128)(2,1)S(1)}, bf16[384,1024]{1,0:T(8,128)(2,1)S(1)}, u32[]{:S(2)}, u32[]{:S(2)}) collective-permute-start(bf16[384,1024]{1,0:T(8,128)(2,1)S(1)} %maximum_convert_fusion.1.refs_0_), channel_id=1, source_target_pairs={{0,4},{1,5},{4,0},{5,1},{2,6},{3,7},{6,2},{7,3},{8,12},{9,13},{12,... | collective-permute-start | bytes 2359304 | tf_op jit(solution)/shard_map/ppermute | solution.py:216
  20.4 1.6 collective-permute-start.5
  22.5 13.7 %collective-permute-done.4.refs_6_ = bf16[384,1024]{1,0:T(8,128)(2,1)S(1)} collective-permute-done((bf16[384,1024]{1,0:T(8,128)(2,1)S(1)}, bf16[384,1024]{1,0:T(8,128)(2,1)S(1)}, u32[]{:S(2)}, u32[]{:S(2)}) %collective-permute-start.4) | collective-permute-done | bytes 786464 | tf_op jit(solution)/shard_map/ppermute | solution.py:216
  36.2 19.0 %collective-permute-done.6.refs_10_ = bf16[384,1024]{1,0:T(8,128)(2,1)S(1)} collective-permute-done((bf16[384,1024]{1,0:T(8,128)(2,1)S(1)}, bf16[384,1024]{1,0:T(8,128)(2,1)S(1)}, u32[]{:S(2)}, u32[]{:S(2)}) %collective-permute-start.6) | collective-permute-done | bytes 786464 | tf_op jit(solution)/shard_map/ppermute | solution.py:216
  56.9 1.3 collective-permute-start.16
  58.2 1.0 collective-permute-done.10.refs_5_
  60.4 4.0 %collective-permute-start.7 = (bf16[384,1024]{1,0:T(8,128)(2,1)S(1)}, bf16[384,1024]{1,0:T(8,128)(2,1)}, u32[]{:S(2)}, u32[]{:S(2)}) collective-permute-start(bf16[384,1024]{1,0:T(8,128)(2,1)S(1)} %maximum_convert_fusion.refs_2_), channel_id=1, source_target_pairs={{0,4},{1,5},{4,0},{5,1},{2,6},{3,7},{6,2},{7,3},{8,12},{9,13},{12,... | collective-permute-start | bytes 2359304 | tf_op jit(solution)/shard_map/ppermute | solution.py:216
  67.0 18.8 %shard_map.64 = (bf16[67,256,512]{2,1,0:T(8,128)(2,1)}, bf16[16,2,384,1024]{3,2,1,0:T(8,128)(2,1)}, s32[1]{0:T(128)}) custom-call(s32[6]{0:T(128)} %stack.72.where_ref, s32[67]{0:T(128)} %select_reduce_fusion.2.order_ref, s32[8]{0:T(128)} %convert_reduce_fusion.1.bound_ref, s32[67]{0:T(128)} %copy-done.26, s32[67]{0:T(128)} %copy-done.25, ...), custom_call_target="tpu_custom_call" | custom-call | flops 1348888192 | bytes 3951820 | tf_op jit(solution)/shard_map/pallas_call | solution.py:140
  85.8 13.6 %collective-permute-done.7.refs_4_ = bf16[384,1024]{1,0:T(8,128)(2,1)} collective-permute-done((bf16[384,1024]{1,0:T(8,128)(2,1)S(1)}, bf16[384,1024]{1,0:T(8,128)(2,1)}, u32[]{:S(2)}, u32[]{:S(2)}) %collective-permute-start.7) | collective-permute-done | bytes 786464 | tf_op jit(solution)/shard_map/ppermute | solution.py:216
  100.7 1.3 collective-permute-start.17
  103.4 0.9 collective-permute-done.19.refs_3_
  105.2 10.3 %shard_map.65 = (bf16[67,256,512]{2,1,0:T(8,128)(2,1)}, bf16[16,2,384,1024]{3,2,1,0:T(8,128)(2,1)}, s32[1]{0:T(128)}) custom-call(s32[3]{0:T(128)} %pad_add_fusion.1.where_ref, s32[67]{0:T(128)} %select_reduce_fusion.2.order_ref, s32[8]{0:T(128)} %convert_reduce_fusion.1.bound_ref, s32[67]{0:T(128)} %copy-done.26, ...), custom_call_target="tpu_custom_call", output_to_operand_aliasing={{0}: (12, {}), {1}: (13, {})} | custom-call | flops 1348888192 | bytes 3951820 | tf_op jit(solution)/shard_map/pallas_call | solution.py:140
  115.5 4.7 %collective-permute-done.21.refs_0_ = bf16[384,1024]{1,0:T(8,128)(2,1)S(1)} collective-permute-done((bf16[384,1024]{1,0:T(8,128)(2,1)}, bf16[384,1024]{1,0:T(8,128)(2,1)S(1)}, u32[]{:S(2)}, u32[]{:S(2)}) %collective-permute-start.21) | collective-permute-done | bytes 786464 | tf_op jit(solution)/shard_map/ppermute | solution.py:216
  120.2 2.1 %collective-permute-done.17 = bf16[384,1024]{1,0:T(8,128)(2,1)S(1)} collective-permute-done((bf16[384,1024]{1,0:T(8,128)(2,1)}, bf16[384,1024]{1,0:T(8,128)(2,1)S(1)}, u32[]{:S(2)}, u32[]{:S(2)}) %collective-permute-start.17) | collective-permute-done | bytes 786464 | tf_op jit(solution)/shard_map/ppermute | solution.py:216
  123.3 1.5 collective-permute-start.26
  124.8 3.5 %collective-permute-start.27 = (bf16[384,1024]{1,0:T(8,128)(2,1)S(1)}, bf16[384,1024]{1,0:T(8,128)(2,1)S(1)}, u32[]{:S(2)}, u32[]{:S(2)}) collective-permute-start(bf16[384,1024]{1,0:T(8,128)(2,1)S(1)} %copy-done.1), channel_id=1, source_target_pairs={{0,2},{1,3},{2,0},{3,1},{4,6},{5,7},{6,4},{7,5},{8,10},{9,11},{10,... | collective-permute-start | bytes 2359304 | tf_op jit(solution)/shard_map/ppermute | solution.py:216
  129.6 0.9 copy-done.13
  130.7 12.0 %shard_map.66 = (bf16[67,256,512]{2,1,0:T(8,128)(2,1)}, bf16[16,2,384,1024]{3,2,1,0:T(8,128)(2,1)}, s32[1]{0:T(128)}) custom-call(s32[2]{0:T(128)} %pad_add_fusion.2.where_ref, s32[67]{0:T(128)} %select_reduce_fusion.2.order_ref, s32[8]{0:T(128)} %convert_reduce_fusion.1.bound_ref, s32[67]{0:T(128)} %copy-done.26, ...), custom_call_target="tpu_custom_call", output_to_operand_aliasing={{0}: (10, {}), {1}: (11, {})} | custom-call | flops 1348888192 | bytes 3951820 | tf_op jit(solution)/shard_map/pallas_call | solution.py:140
  142.8 3.0 %collective-permute-done.27.refs_4_ = bf16[384,1024]{1,0:T(8,128)(2,1)S(1)} collective-permute-done((bf16[384,1024]{1,0:T(8,128)(2,1)S(1)}, bf16[384,1024]{1,0:T(8,128)(2,1)S(1)}, u32[]{:S(2)}, u32[]{:S(2)}) %collective-permute-start.27) | collective-permute-done | bytes 786464 | tf_op jit(solution)/shard_map/ppermute | solution.py:216
  147.3 3.6 %collective-permute-start.32 = (bf16[384,1024]{1,0:T(8,128)(2,1)S(1)}, bf16[384,1024]{1,0:T(8,128)(2,1)S(1)}, u32[]{:S(2)}, u32[]{:S(2)}) collective-permute-start(bf16[384,1024]{1,0:T(8,128)(2,1)S(1)} %copy-done.8), channel_id=1, source_target_pairs={{0,2},{1,3},{2,0},{3,1},{4,6},{5,7},{6,4},{7,5},{8,10},{9,11},{10,... | collective-permute-start | bytes 2359304 | tf_op jit(solution)/shard_map/ppermute | solution.py:216
  153.0 18.0 %shard_map.67 = (bf16[67,256,512]{2,1,0:T(8,128)(2,1)}, bf16[16,2,384,1024]{3,2,1,0:T(8,128)(2,1)}, s32[1]{0:T(128)}) custom-call(s32[3]{0:T(128)} %pad_add_fusion.3.where_ref, s32[67]{0:T(128)} %select_reduce_fusion.2.order_ref, s32[8]{0:T(128)} %convert_reduce_fusion.1.bound_ref, s32[67]{0:T(128)} %copy-done.26, ...), custom_call_target="tpu_custom_call", output_to_operand_aliasing={{0}: (12, {}), {1}: (13, {})} | custom-call | flops 1348888192 | bytes 3951820 | tf_op jit(solution)/shard_map/pallas_call | solution.py:140
  172.2 1.2 collective-permute-done.33.refs_1_
  173.4 1.1 collective-permute-done.34.refs_3_
  174.5 0.9 copy-done.16
  175.4 14.3 %shard_map.68 = (bf16[67,256,512]{2,1,0:T(8,128)(2,1)}, bf16[16,2,384,1024]{3,2,1,0:T(8,128)(2,1)}, s32[1]{0:T(128)}) custom-call(s32[2]{0:T(128)} %pad_add_fusion.where_ref, s32[67]{0:T(128)} %select_reduce_fusion.2.order_ref, s32[8]{0:T(128)} %convert_reduce_fusion.1.bound_ref, s32[67]{0:T(128)} %copy-done.26, ...), custom_call_target="tpu_custom_call", output_to_operand_aliasing={{0}: (10, {}), {1}: (11, {})} | custom-call | flops 1348888192 | bytes 3951820 | tf_op jit(solution)/shard_map/pallas_call | solution.py:140
  (134 shorter events, 18.6 us)
Async XLA Ops:
  2.1 6.6 %collective-permute-start = (bf16[384,1792]{1,0:T(8,128)(2,1)S(1)}, bf16[384,1792]{1,0:T(8,128)(2,1)S(1)}, u32[]{:S(2)}, u32[]{:S(2)}) collective-permute-start(bf16[384,1792]{1,0:T(8,128)(2,1)S(1)} %broadcast_select_fusion), channel_id=1, source_target_pairs={{0,8},{8,0},{1,9},{9,1},{2,10},{10,2},{3,11},{11,3},{4,12},{12,4},... | collective-permute-start | bytes 4128776 | tf_op jit(solution)/shard_map/ppermute | solution.py:311
  15.1 21.1 %collective-permute-start.4 = (bf16[384,1024]{1,0:T(8,128)(2,1)S(1)}, bf16[384,1024]{1,0:T(8,128)(2,1)S(1)}, u32[]{:S(2)}, u32[]{:S(2)}) collective-permute-start(bf16[384,1024]{1,0:T(8,128)(2,1)S(1)} %maximum_convert_fusion.refs_2_), channel_id=1, source_target_pairs={{0,1},{1,0},{2,3},{3,2},{4,5},{5,4},{6,7},{7,6},{8,9},{9,8},{10,11... | collective-permute-start | bytes 2359304 | tf_op jit(solution)/shard_map/ppermute | solution.py:216
  17.8 37.4 %collective-permute-start.6 = (bf16[384,1024]{1,0:T(8,128)(2,1)S(1)}, bf16[384,1024]{1,0:T(8,128)(2,1)S(1)}, u32[]{:S(2)}, u32[]{:S(2)}) collective-permute-start(bf16[384,1024]{1,0:T(8,128)(2,1)S(1)} %maximum_convert_fusion.1.refs_0_), channel_id=1, source_target_pairs={{0,4},{1,5},{4,0},{5,1},{2,6},{3,7},{6,2},{7,3},{8,12},{9,13},{12,... | collective-permute-start | bytes 2359304 | tf_op jit(solution)/shard_map/ppermute | solution.py:216
  20.4 35.1 %collective-permute-start.5 = (bf16[384,1024]{1,0:T(8,128)(2,1)S(1)}, bf16[384,1024]{1,0:T(8,128)(2,1)}, u32[]{:S(2)}, u32[]{:S(2)}) collective-permute-start(bf16[384,1024]{1,0:T(8,128)(2,1)S(1)} %maximum_convert_fusion.1.refs_0_), channel_id=1, source_target_pairs={{0,2},{1,3},{2,0},{3,1},{4,6},{5,7},{6,4},{7,5},{8,10},{9,11},{10,... | collective-permute-start | bytes 2359304 | tf_op jit(solution)/shard_map/ppermute | solution.py:216
  22.0 33.5 %collective-permute-start.3 = (bf16[384,1024]{1,0:T(8,128)(2,1)S(1)}, bf16[384,1024]{1,0:T(8,128)(2,1)}, u32[]{:S(2)}, u32[]{:S(2)}) collective-permute-start(bf16[384,1024]{1,0:T(8,128)(2,1)S(1)} %maximum_convert_fusion.1.refs_0_), channel_id=1, source_target_pairs={{0,1},{1,0},{2,3},{3,2},{4,5},{5,4},{6,7},{7,6},{8,9},{9,8},{10,11... | collective-permute-start | bytes 2359304 | tf_op jit(solution)/shard_map/ppermute | solution.py:216
  22.5 33.9 %collective-permute-start.9 = (bf16[384,1024]{1,0:T(8,128)(2,1)S(1)}, bf16[384,1024]{1,0:T(8,128)(2,1)}, u32[]{:S(2)}, u32[]{:S(2)}) collective-permute-start(bf16[384,1024]{1,0:T(8,128)(2,1)S(1)} %maximum_convert_fusion.refs_2_), channel_id=1, source_target_pairs={{0,8},{8,0},{1,9},{9,1},{2,10},{10,2},{3,11},{11,3},{4,12},{12,4},... | collective-permute-start | bytes 2359304 | tf_op jit(solution)/shard_map/ppermute | solution.py:216
  36.2 20.7 %collective-permute-start.8 = (bf16[384,1024]{1,0:T(8,128)(2,1)S(1)}, bf16[384,1024]{1,0:T(8,128)(2,1)}, u32[]{:S(2)}, u32[]{:S(2)}) collective-permute-start(bf16[384,1024]{1,0:T(8,128)(2,1)S(1)} %maximum_convert_fusion.1.refs_0_), channel_id=1, source_target_pairs={{0,8},{8,0},{1,9},{9,1},{2,10},{10,2},{3,11},{11,3},{4,12},{12,4},... | collective-permute-start | bytes 2359304 | tf_op jit(solution)/shard_map/ppermute | solution.py:216
  55.5 3.7 %collective-permute-start.10 = (bf16[384,1024]{1,0:T(8,128)(2,1)}, bf16[384,1024]{1,0:T(8,128)(2,1)}, u32[]{:S(2)}, u32[]{:S(2)}) collective-permute-start(bf16[384,1024]{1,0:T(8,128)(2,1)} %collective-permute-done.3.refs_4_), channel_id=1, source_target_pairs={{0,8},{8,0},{1,9},{9,1},{2,10},{10,2},{3,11},{11,3},{4,12},{12,4},... | collective-permute-start | bytes 2359304 | tf_op jit(solution)/shard_map/ppermute | solution.py:216
  55.5 4.3 %collective-permute-start.11 = (bf16[384,1024]{1,0:T(8,128)(2,1)S(1)}, bf16[384,1024]{1,0:T(8,128)(2,1)}, u32[]{:S(2)}, u32[]{:S(2)}) collective-permute-start(bf16[384,1024]{1,0:T(8,128)(2,1)S(1)} %collective-permute-done.4.refs_6_), channel_id=1, source_target_pairs={{0,8},{8,0},{1,9},{9,1},{2,10},{10,2},{3,11},{11,3},{4,12},{12,4},... | collective-permute-start | bytes 2359304 | tf_op jit(solution)/shard_map/ppermute | solution.py:216
  56.0 4.4 %collective-permute-start.12 = (bf16[384,1024]{1,0:T(8,128)(2,1)}, bf16[384,1024]{1,0:T(8,128)(2,1)}, u32[]{:S(2)}, u32[]{:S(2)}) collective-permute-start(bf16[384,1024]{1,0:T(8,128)(2,1)} %collective-permute-done.5.refs_8_), channel_id=1, source_target_pairs={{0,8},{8,0},{1,9},{9,1},{2,10},{10,2},{3,11},{11,3},{4,12},{12,4},... | collective-permute-start | bytes 2359304 | tf_op jit(solution)/shard_map/ppermute | solution.py:216
  56.4 43.1 %collective-permute-start.14 = (bf16[384,1024]{1,0:T(8,128)(2,1)}, bf16[384,1024]{1,0:T(8,128)(2,1)}, u32[]{:S(2)}, u32[]{:S(2)}) collective-permute-start(bf16[384,1024]{1,0:T(8,128)(2,1)} %collective-permute-done.5.refs_8_), channel_id=1, source_target_pairs={{0,1},{1,0},{2,3},{3,2},{4,5},{5,4},{6,7},{7,6},{8,9},{9,8},{10,11... | collective-permute-start | bytes 2359304 | tf_op jit(solution)/shard_map/ppermute | solution.py:216
  56.9 42.6 %collective-permute-start.16 = (bf16[384,1024]{1,0:T(8,128)(2,1)S(1)}, bf16[384,1024]{1,0:T(8,128)(2,1)S(1)}, u32[]{:S(2)}, u32[]{:S(2)}) collective-permute-start(bf16[384,1024]{1,0:T(8,128)(2,1)S(1)} %collective-permute-done.6.refs_10_), channel_id=1, source_target_pairs={{2,0},{3,1},{4,6},{5,7},{10,8},{11,9},{12,14},{13,15},{18,16},{19,... | collective-permute-start | bytes 2359304 | tf_op jit(solution)/shard_map/ppermute | solution.py:216
  59.2 40.3 %collective-permute-start.15 = (bf16[384,1024]{1,0:T(8,128)(2,1)S(1)}, bf16[384,1024]{1,0:T(8,128)(2,1)}, u32[]{:S(2)}, u32[]{:S(2)}) collective-permute-start(bf16[384,1024]{1,0:T(8,128)(2,1)S(1)} %collective-permute-done.6.refs_10_), channel_id=1, source_target_pairs={{0,1},{1,0},{2,3},{3,2},{4,5},{5,4},{6,7},{7,6},{8,9},{9,8},{10,11... | collective-permute-start | bytes 2359304 | tf_op jit(solution)/shard_map/ppermute | solution.py:216
  59.8 7.2 %collective-permute-start.13 = (bf16[384,1024]{1,0:T(8,128)(2,1)S(1)}, bf16[384,1024]{1,0:T(8,128)(2,1)}, u32[]{:S(2)}, u32[]{:S(2)}) collective-permute-start(bf16[384,1024]{1,0:T(8,128)(2,1)S(1)} %collective-permute-done.6.refs_10_), channel_id=1, source_target_pairs={{0,8},{8,0},{1,9},{9,1},{2,10},{10,2},{3,11},{11,3},{4,12},{12,4},... | collective-permute-start | bytes 2359304 | tf_op jit(solution)/shard_map/ppermute | solution.py:216
  60.4 39.1 %collective-permute-start.7 = (bf16[384,1024]{1,0:T(8,128)(2,1)S(1)}, bf16[384,1024]{1,0:T(8,128)(2,1)}, u32[]{:S(2)}, u32[]{:S(2)}) collective-permute-start(bf16[384,1024]{1,0:T(8,128)(2,1)S(1)} %maximum_convert_fusion.refs_2_), channel_id=1, source_target_pairs={{0,4},{1,5},{4,0},{5,1},{2,6},{3,7},{6,2},{7,3},{8,12},{9,13},{12,... | collective-permute-start | bytes 2359304 | tf_op jit(solution)/shard_map/ppermute | solution.py:216
  99.5 2.6 %collective-permute-start.20 = (bf16[384,1024]{1,0:T(8,128)(2,1)}, bf16[384,1024]{1,0:T(8,128)(2,1)S(1)}, u32[]{:S(2)}, u32[]{:S(2)}) collective-permute-start(bf16[384,1024]{1,0:T(8,128)(2,1)} %collective-permute-done.7.refs_4_), channel_id=1, source_target_pairs={{0,8},{8,0},{1,9},{9,1},{2,10},{10,2},{3,11},{11,3},{4,12},{12,4},... | collective-permute-start | bytes 2359304 | tf_op jit(solution)/shard_map/ppermute | solution.py:216
  99.6 3.8 %collective-permute-start.18 = (bf16[384,1024]{1,0:T(8,128)(2,1)}, bf16[384,1024]{1,0:T(8,128)(2,1)S(1)}, u32[]{:S(2)}, u32[]{:S(2)}) collective-permute-start(bf16[384,1024]{1,0:T(8,128)(2,1)} %collective-permute-done.14.refs_0_), channel_id=1, source_target_pairs={{0,8},{8,0},{1,9},{9,1},{2,10},{10,2},{3,11},{11,3},{4,12},{12,4},... | collective-permute-start | bytes 2359304 | tf_op jit(solution)/shard_map/ppermute | solution.py:216
  100.1 4.2 %collective-permute-start.19 = (bf16[384,1024]{1,0:T(8,128)(2,1)}, bf16[384,1024]{1,0:T(8,128)(2,1)S(1)}, u32[]{:S(2)}, u32[]{:S(2)}) collective-permute-start(bf16[384,1024]{1,0:T(8,128)(2,1)} %collective-permute-done.15.refs_2_), channel_id=1, source_target_pairs={{0,8},{8,0},{1,9},{9,1},{2,10},{10,2},{3,11},{11,3},{4,12},{12,4},... | collective-permute-start | bytes 2359304 | tf_op jit(solution)/shard_map/ppermute | solution.py:216
  100.1 20.1 %collective-permute-start.21 = (bf16[384,1024]{1,0:T(8,128)(2,1)}, bf16[384,1024]{1,0:T(8,128)(2,1)S(1)}, u32[]{:S(2)}, u32[]{:S(2)}) collective-permute-start(bf16[384,1024]{1,0:T(8,128)(2,1)} %collective-permute-done.7.refs_4_), channel_id=1, source_target_pairs={{0,1},{1,0},{2,3},{3,2},{4,5},{5,4},{6,7},{7,6},{8,9},{9,8},{10,11... | collective-permute-start | bytes 2359304 | tf_op jit(solution)/shard_map/ppermute | solution.py:216
  100.7 21.7 %collective-permute-start.17 = (bf16[384,1024]{1,0:T(8,128)(2,1)}, bf16[384,1024]{1,0:T(8,128)(2,1)S(1)}, u32[]{:S(2)}, u32[]{:S(2)}) collective-permute-start(bf16[384,1024]{1,0:T(8,128)(2,1)} %collective-permute-done.7.refs_4_), channel_id=1, source_target_pairs={{2,0},{3,1},{4,6},{5,7},{10,8},{11,9},{12,14},{13,15},{18,16},{19,... | collective-permute-start | bytes 2359304 | tf_op jit(solution)/shard_map/ppermute | solution.py:216
  102.0 20.3 %collective-permute-start.22 = (bf16[384,1024]{1,0:T(8,128)(2,1)S(1)}, bf16[384,1024]{1,0:T(8,128)(2,1)S(1)}, u32[]{:S(2)}, u32[]{:S(2)}) collective-permute-start(bf16[384,1024]{1,0:T(8,128)(2,1)S(1)} %copy-done.3), channel_id=1, source_target_pairs={{2,4},{3,5},{4,2},{5,3},{10,12},{11,13},{12,10},{13,11},{18,20},{1... | collective-permute-start | bytes 2359304 | tf_op jit(solution)/shard_map/ppermute | solution.py:216
  122.7 6.9 %collective-permute-start.25 = (bf16[384,1024]{1,0:T(8,128)(2,1)S(1)}, bf16[384,1024]{1,0:T(8,128)(2,1)S(1)}, u32[]{:S(2)}, u32[]{:S(2)}) collective-permute-start(bf16[384,1024]{1,0:T(8,128)(2,1)S(1)} %add.165.refs_2_), channel_id=1, source_target_pairs={{0,8},{8,0},{1,9},{9,1},{2,10},{10,2},{3,11},{11,3},{4,12},{12,4},... | collective-permute-start | bytes 2359304 | tf_op jit(solution)/shard_map/ppermute | solution.py:216
  122.8 6.8 %collective-permute-start.24 = (bf16[384,1024]{1,0:T(8,128)(2,1)S(1)}, bf16[384,1024]{1,0:T(8,128)(2,1)S(1)}, u32[]{:S(2)}, u32[]{:S(2)}) collective-permute-start(bf16[384,1024]{1,0:T(8,128)(2,1)S(1)} %collective-permute-done.21.refs_0_), channel_id=1, source_target_pairs={{0,8},{8,0},{1,9},{9,1},{2,10},{10,2},{3,11},{11,3},{4,12},{12,4},... | collective-permute-start | bytes 2359304 | tf_op jit(solution)/shard_map/ppermute | solution.py:216
  123.3 19.5 %collective-permute-start.26 = (bf16[384,1024]{1,0:T(8,128)(2,1)S(1)}, bf16[384,1024]{1,0:T(8,128)(2,1)S(1)}, u32[]{:S(2)}, u32[]{:S(2)}) collective-permute-start(bf16[384,1024]{1,0:T(8,128)(2,1)S(1)} %add.165.refs_2_), channel_id=1, source_target_pairs={{0,1},{1,0},{2,3},{3,2},{4,5},{5,4},{6,7},{7,6},{8,9},{9,8},{10,11... | collective-permute-start | bytes 2359304 | tf_op jit(solution)/shard_map/ppermute | solution.py:216
  124.8 21.0 %collective-permute-start.27 = (bf16[384,1024]{1,0:T(8,128)(2,1)S(1)}, bf16[384,1024]{1,0:T(8,128)(2,1)S(1)}, u32[]{:S(2)}, u32[]{:S(2)}) collective-permute-start(bf16[384,1024]{1,0:T(8,128)(2,1)S(1)} %copy-done.1), channel_id=1, source_target_pairs={{0,2},{1,3},{2,0},{3,1},{4,6},{5,7},{6,4},{7,5},{8,10},{9,11},{10,... | collective-permute-start | bytes 2359304 | tf_op jit(solution)/shard_map/ppermute | solution.py:216
  128.3 17.5 %collective-permute-start.23 = (bf16[384,1024]{1,0:T(8,128)(2,1)S(1)}, bf16[384,1024]{1,0:T(8,128)(2,1)S(1)}, u32[]{:S(2)}, u32[]{:S(2)}) collective-permute-start(bf16[384,1024]{1,0:T(8,128)(2,1)S(1)} %copy-done.1), channel_id=1, source_target_pairs={{2,4},{3,5},{4,2},{5,3},{10,12},{11,13},{12,10},{13,11},{18,20},{1... | collective-permute-start | bytes 2359304 | tf_op jit(solution)/shard_map/ppermute | solution.py:216
  146.1 5.4 %collective-permute-start.30 = (bf16[384,1024]{1,0:T(8,128)(2,1)S(1)}, bf16[384,1024]{1,0:T(8,128)(2,1)S(1)}, u32[]{:S(2)}, u32[]{:S(2)}) collective-permute-start(bf16[384,1024]{1,0:T(8,128)(2,1)S(1)} %add.164.refs_2_), channel_id=1, source_target_pairs={{0,8},{8,0},{1,9},{9,1},{2,10},{10,2},{3,11},{11,3},{4,12},{12,4},... | collective-permute-start | bytes 2359304 | tf_op jit(solution)/shard_map/ppermute | solution.py:216
  146.2 5.4 %collective-permute-start.29 = (bf16[384,1024]{1,0:T(8,128)(2,1)S(1)}, bf16[384,1024]{1,0:T(8,128)(2,1)S(1)}, u32[]{:S(2)}, u32[]{:S(2)}) collective-permute-start(bf16[384,1024]{1,0:T(8,128)(2,1)S(1)} %collective-permute-done.26.refs_0_), channel_id=1, source_target_pairs={{0,8},{8,0},{1,9},{9,1},{2,10},{10,2},{3,11},{11,3},{4,12},{12,4},... | collective-permute-start | bytes 2359304 | tf_op jit(solution)/shard_map/ppermute | solution.py:216
  146.7 4.9 %collective-permute-start.31 = (bf16[384,1024]{1,0:T(8,128)(2,1)S(1)}, bf16[384,1024]{1,0:T(8,128)(2,1)S(1)}, u32[]{:S(2)}, u32[]{:S(2)}) collective-permute-start(bf16[384,1024]{1,0:T(8,128)(2,1)S(1)} %collective-permute-done.27.refs_4_), channel_id=1, source_target_pairs={{0,8},{8,0},{1,9},{9,1},{2,10},{10,2},{3,11},{11,3},{4,12},{12,4},... | collective-permute-start | bytes 2359304 | tf_op jit(solution)/shard_map/ppermute | solution.py:216
  146.8 24.2 %collective-permute-start.28 = (bf16[384,1024]{1,0:T(8,128)(2,1)S(1)}, bf16[384,1024]{1,0:T(8,128)(2,1)S(1)}, u32[]{:S(2)}, u32[]{:S(2)}) collective-permute-start(bf16[384,1024]{1,0:T(8,128)(2,1)S(1)} %add.164.refs_2_), channel_id=1, source_target_pairs={{0,1},{1,0},{2,3},{3,2},{4,5},{5,4},{6,7},{7,6},{8,9},{9,8},{10,11... | collective-permute-start | bytes 2359304 | tf_op jit(solution)/shard_map/ppermute | solution.py:216
  147.3 23.7 %collective-permute-start.32 = (bf16[384,1024]{1,0:T(8,128)(2,1)S(1)}, bf16[384,1024]{1,0:T(8,128)(2,1)S(1)}, u32[]{:S(2)}, u32[]{:S(2)}) collective-permute-start(bf16[384,1024]{1,0:T(8,128)(2,1)S(1)} %copy-done.8), channel_id=1, source_target_pairs={{0,2},{1,3},{2,0},{3,1},{4,6},{5,7},{6,4},{7,5},{8,10},{9,11},{10,... | collective-permute-start | bytes 2359304 | tf_op jit(solution)/shard_map/ppermute | solution.py:216
  171.1 3.4 %collective-permute-start.34 = (bf16[384,1024]{1,0:T(8,128)(2,1)S(1)}, bf16[384,1024]{1,0:T(8,128)(2,1)S(1)}, u32[]{:S(2)}, u32[]{:S(2)}) collective-permute-start(bf16[384,1024]{1,0:T(8,128)(2,1)S(1)} %collective-permute-done.32.refs_2_), channel_id=1, source_target_pairs={{0,8},{8,0},{1,9},{9,1},{2,10},{10,2},{3,11},{11,3},{4,12},{12,4},... | collective-permute-start | bytes 2359304 | tf_op jit(solution)/shard_map/ppermute | solution.py:216
  (36 other events, 390.8 us)

commit v2 on v1

v2 whole, which is shorter than its diff:
```python
import functools

import jax
import jax.numpy as jnp
import numpy as np
from jax import lax
from jax.experimental import pallas as pl
from jax.experimental.pallas import tpu as pltpu
from jax.sharding import PartitionSpec as P

F = 16384
TILE = 512
ABREAST = 4


def tile_tables(block_count):
    row_list = []
    col_list = []
    for row_block in range(block_count):
        for col_block in range(row_block, block_count):
            row_list.append(row_block)
            col_list.append(col_block)
    row_list.append(0)
    col_list.append(0)
    return (np.array(row_list, np.int32), np.array(col_list, np.int32))


def block_ids(table, tile_total, row_table, col_table):
    matches = table[:, None] == jnp.arange(tile_total + 1, dtype=jnp.int32)[None, :]
    row_ids = jnp.sum(jnp.where(matches, jnp.asarray(row_table)[None, :], 0), axis=1).astype(
        jnp.int32
    )
    col_ids = jnp.sum(jnp.where(matches, jnp.asarray(col_table)[None, :], 0), axis=1).astype(
        jnp.int32
    )
    return (row_ids, col_ids)


def slot_tables(owner, tokens):
    block_count = F // TILE
    tile_total = block_count * (block_count + 1) // 2
    row_table, col_table = tile_tables(block_count)
    row_ids, col_ids = block_ids(owner, tile_total, row_table, col_table)
    slot_scale = (owner < tile_total).astype(jnp.float32) / tokens
    return row_ids, col_ids, slot_scale


def tiles_kernel(sources, count, held, stage, lead, final, *refs):
    where_ref, order_ref, bound_ref, row_ref, col_ref, scale_ref, age_ref, near_ref = refs[:8]
    pieces = refs[8 : 8 + count]
    out_ref, codes, done_ref, pool, out_buf, in_sem, keep_sem, load_sem, out_sem = refs[
        8 + count + held :
    ]
    rows = out_ref.shape[1]
    tokens = codes.shape[2]
    half_blocks = pieces[0].shape[1] // TILE
    fresh = len(sources) // 2 * half_blocks
    ring = pool.shape[0] - fresh
    first = bound_ref[stage]
    last = bound_ref[stage + 1]
    my_row = pl.multiple_of(lax.axis_index("tok") * rows, rows)

    arrivals, keeps = [], []
    for idx, (source, row) in enumerate(sources):
        for k in range(half_blocks):
            piece = pieces[source].at[pl.ds(row * tokens, tokens), pl.ds(k * TILE, TILE)]
            here = pool.at[idx // 2 * half_blocks + k, idx % 2]
            there = codes.at[where_ref[lead + idx // 2] * half_blocks + k, idx % 2]
            arrivals.append(pltpu.make_async_copy(piece, here, in_sem.at[idx, k]))
            if not final:
                keeps.append(pltpu.make_async_copy(here, there, keep_sem.at[idx, k]))
    for c in arrivals:
        c.start()

    def slot_of(t):
        return lax.rem(t - first, ring)

    def load(t, go):
        slot = order_ref[jnp.minimum(t, order_ref.shape[0] - 1)]
        row_blk = row_ref[slot]
        col_blk = col_ref[slot]
        buf = slot_of(t)

        @pl.when((t < last) & (age_ref[row_blk] != stage))
        def _():
            go(
                pltpu.make_async_copy(
                    codes.at[row_blk, :, :, pl.ds(my_row, rows)],
                    pool.at[fresh + buf, :, :, pl.ds(my_row, rows)],
                    load_sem.at[buf],
                )
            )

        @pl.when((t < last) & (age_ref[col_blk] != stage))
        def _():
            go(pltpu.make_async_copy(codes.at[col_blk], pool.at[fresh + buf], load_sem.at[buf]))

    def store(t, buf, go):
        @pl.when(t < last)
        def _():
            go(pltpu.make_async_copy(out_buf.at[buf], out_ref.at[order_ref[t]], out_sem.at[buf]))

    start = lambda c: c.start()
    wait = lambda c: c.wait()
    for k in range(2 * ABREAST):
        load(first + k, start)
    for c in arrivals:
        c.wait()
    for c in keeps:
        c.start()

    def operands(t):
        slot = order_ref[jnp.minimum(t, last - 1)]
        row_blk = row_ref[slot]
        col_blk = col_ref[slot]
        loaded = fresh + slot_of(t)
        row_at = jnp.where(age_ref[row_blk] == stage, near_ref[row_blk], loaded)
        col_at = jnp.where(age_ref[col_blk] == stage, near_ref[col_blk], loaded)
        return row_at, col_at, scale_ref[slot]

    def some(g, carry):
        t0 = first + g * ABREAST
        side = lax.rem(g, 2) * ABREAST
        for u in range(ABREAST):
            load(t0 + 2 * ABREAST + u, start)
        for u in range(ABREAST):
            load(t0 + u, wait)

        @pl.when(g >= 2)
        def _():
            for u in range(ABREAST):
                store(t0 - 2 * ABREAST + u, side + u, wait)

        for u in range(ABREAST):
            row_at, col_at, scale = operands(t0 + u)
            tile = lax.dot_general(
                pool[row_at, :, :, pl.ds(my_row, rows)].reshape(2 * tokens, rows),
                pool[col_at].reshape(2 * tokens, TILE),
                (((0,), (0,)), ((), ())),
                preferred_element_type=jnp.float32,
            )
            out_buf[side + u] = (tile * scale).astype(out_buf.dtype)
        for u in range(ABREAST):
            store(t0 + u, side + u, start)
        return carry

    groups = lax.div(last - first + ABREAST - 1, ABREAST)
    lax.fori_loop(0, groups, some, 0)
    done_ref[0] = last
    for back in (2, 1):

        @pl.when(groups >= back)
        def _():
            for u in range(ABREAST):
                g = groups - back
                store(first + g * ABREAST + u, lax.rem(g, 2) * ABREAST + u, wait)

    for c in keeps:
        c.wait()


def tiles(stage, lead, final, kept, state, shapes, tables):
    pieces, sources = [], []
    for own, far, row in kept:
        for array, at in ((own, 0), (far, row)):
            known = [k for k, piece in enumerate(pieces) if piece is array]
            if not known:
                pieces.append(array)
            sources.append((known[0] if known else len(pieces) - 1, at))
    out, codes = shapes
    slots, rows, _ = out.shape
    half_blocks = pieces[0].shape[1] // TILE
    smem = pl.BlockSpec(memory_space=pltpu.SMEM)
    anywhere = pl.BlockSpec(memory_space=pl.ANY)
    before = len(tables) + len(pieces)
    return pl.pallas_call(
        functools.partial(
            tiles_kernel, tuple(sources), len(pieces), len(state), stage, lead, final
        ),
        out_shape=[out, codes, jax.ShapeDtypeStruct((1,), jnp.int32)],
        in_specs=[smem] * len(tables) + [anywhere] * (len(pieces) + len(state)),
        out_specs=[anywhere, anywhere, smem],
        input_output_aliases={before + k: k for k in range(len(state))},
        scratch_shapes=[
            pltpu.VMEM((len(kept) * half_blocks + 3 * ABREAST, *codes.shape[1:]), codes.dtype),
            pltpu.VMEM((2 * ABREAST, rows, TILE), out.dtype),
            pltpu.SemaphoreType.DMA((len(sources), half_blocks)),
            pltpu.SemaphoreType.DMA((len(sources), half_blocks)),
            pltpu.SemaphoreType.DMA((3 * ABREAST,)),
            pltpu.SemaphoreType.DMA((2 * ABREAST,)),
        ],
        compiler_params=pltpu.CompilerParams(vmem_limit_bytes=32 * 1024 * 1024),
        cost_estimate=pl.CostEstimate(flops=1000, bytes_accessed=1000, transcendentals=0),
    )(*tables, *pieces, *state)


def stage_tables(row_ids, col_ids, age):
    slots = row_ids.shape[0]
    block = jnp.arange(age.shape[0], dtype=jnp.int32)[None, :]
    pick = lambda ids: jnp.sum(jnp.where(ids[:, None] == block, age[None, :], 0), axis=1)
    stage = jnp.maximum(pick(row_ids), pick(col_ids))
    idx = jnp.arange(slots, dtype=jnp.int32)
    key = stage * slots + idx
    rank = jnp.sum((key[None, :] < key[:, None]).astype(jnp.int32), axis=1)
    order = jnp.sum(jnp.where(rank[None, :] == idx[:, None], idx[None, :], 0), axis=1)
    bounds = jnp.sum(
        (stage[None, :] < jnp.arange(8, dtype=jnp.int32)[:, None]).astype(jnp.int32), axis=1
    )
    return order.astype(jnp.int32), bounds.astype(jnp.int32)


def dev(z, x):
    return z * 2 + x


def z_pairs(moves):
    return [(dev(s, x), dev(d, x)) for s, d in moves for x in range(2)]


SWAP = [(0, 1), (1, 0)]
ACROSS = [(dev(z, x), dev(z, 1 - x)) for z in range(4) for x in range(2)]
NEXT = z_pairs([(0, 1), (1, 0), (2, 3), (3, 2)])
SECOND = z_pairs([(0, 2), (2, 0), (1, 3), (3, 1)])
MIDDLE = z_pairs([(1, 2), (2, 1)])
OUTWARD = z_pairs([(1, 0), (2, 3)])

STAGES = (
    ((0, 0, 0), (0, 0, 1), (0, 1, 0), (0, 1, 1), (1, 0, 0), (2, 0, 0)),
    ((1, 1, 0), (2, 1, 0), (2, 0, 1)),
    ((2, 1, 1), (3, 0, 0)),
    ((3, 1, 0), (3, 0, 1), (1, 0, 1)),
    ((3, 1, 1), (1, 1, 1)),
)


class Mover:
    def __init__(self, base):
        self.base = base
        self.seen = ()
        self.pieces = {}

    def after(self, *arrays):
        self.seen = self.seen + arrays

    def send(self, array, pairs, axis="feat", early=0):
        if self.seen:
            array = lax.optimization_barrier((array,) + self.seen)[0]
        for _ in range(early):
            array = lax.optimization_barrier((array, self.base))[0]
        return lax.ppermute(array, axis, pairs)

    def keep(self, **arrays):
        group = tuple(arrays.values())
        joined = jnp.concatenate(group, axis=0) if len(group) > 1 else group[0]
        far = self.send(joined, SWAP, "tok")
        for row, (name, array) in enumerate(arrays.items()):
            self.pieces[tuple(map(int, name[1:]))] = (array, far, row)
        return far


def half_at(me, key):
    z, x, half = key
    return (me ^ (2 * z + x)) * 2 + half


def gather_and_tile(a, b, owner, row_ids, col_ids, slot_scale):
    me = lax.axis_index("feat")
    tokens, width = a.shape
    half_blocks = width // TILE
    block = jnp.arange(F // TILE, dtype=jnp.int32)
    age, near = jnp.zeros_like(block), jnp.zeros_like(block)
    for stage, keys in enumerate(STAGES):
        for at, key in enumerate(keys):
            mine = block // half_blocks == half_at(me, key)
            age = jnp.where(mine, stage, age)
            near = jnp.where(mine, at * half_blocks + block % half_blocks, near)
    order, bounds = stage_tables(row_ids, col_ids, age)
    where = jnp.stack([half_at(me, key) for keys in STAGES for key in keys]).astype(jnp.int32)
    tables = (where, order, bounds, row_ids, col_ids, slot_scale, age, near)
    shapes = (
        jax.ShapeDtypeStruct((row_ids.shape[0], TILE // lax.axis_size("tok"), TILE), a.dtype),
        jax.ShapeDtypeStruct((F // TILE, 2, tokens, TILE), a.dtype),
    )
    m = Mover(owner)

    def work(stage, state):
        kept = [m.pieces[key] for key in STAGES[stage]]
        lead = sum(len(keys) for keys in STAGES[:stage])
        final = stage == len(STAGES) - 1
        *state, done = tiles(stage, lead, final, kept, state, shapes, tables)
        m.after(done)
        return state

    x0a = m.send(a, ACROSS, early=1)
    n1a = m.send(a, NEXT)
    n2a = m.send(a, SECOND, early=1)
    x0b = m.send(b, ACROSS)
    ta = m.keep(p000=a)
    tb = m.keep(p001=b)

    m.after(x0a, x0b, n1a, n2a, ta, tb, *tables)
    x1a = m.send(n1a, ACROSS)
    x2a = m.send(n2a, ACROSS)
    n2b = m.send(b, SECOND)
    fa = m.send(n2a, OUTWARD)
    m.keep(p010=x0a, p011=x0b, p100=n1a, p200=n2a)
    state = work(0, [])

    m.after(x1a, x2a, n2b, fa)
    x2b = m.send(n2b, ACROSS, early=1)
    ga = m.send(a, MIDDLE, early=1)
    fb = m.send(n2b, OUTWARD, early=1)
    m.keep(p110=x1a)
    m.keep(p210=x2a)
    m.keep(p201=n2b)
    state = work(1, state)

    m.after(x2b, ga, fb)
    n3a = fa + ga
    x3a = m.send(n3a, ACROSS, early=1)
    gb = m.send(b, MIDDLE, early=1)
    n1b = m.send(b, NEXT)
    m.keep(p211=x2b)
    m.keep(p300=n3a)
    state = work(2, state)

    m.after(x3a, gb, n1b)
    n3b = fb + gb
    x3b = m.send(n3b, ACROSS, early=1)
    x1b = m.send(x0b, NEXT)
    m.keep(p310=x3a)
    m.keep(p301=n3b)
    m.keep(p101=n1b)
    state = work(3, state)

    m.after(x3b, x1b)
    m.keep(p311=x3b)
    m.keep(p111=x1b)
    return work(4, state)[0]


def encode(inputs, enc_weight, enc_bias):
    batches, tok_rows, model_width = inputs.shape
    flat = inputs.reshape(batches * tok_rows, model_width)
    depth, features = enc_weight.shape
    first = lax.axis_index("tok") == 0
    lower, upper = flat[:, :depth], flat[:, depth:]
    theirs = jnp.where(first, upper, lower)
    other = lax.ppermute(theirs, "tok", SWAP)
    mine = jnp.where(first, lower, upper)
    halves = [slice(k * features // 2, (k + 1) * features // 2) for k in range(2)]
    order = (1, 0)
    near, far, codes = {}, {}, {}
    dot = functools.partial(jnp.dot, preferred_element_type=jnp.float32)
    near[order[0]] = dot(mine, enc_weight[:, halves[order[0]]])
    other = lax.optimization_barrier((other, near[order[0]]))[0]
    for k in order:
        if far:
            other = lax.optimization_barrier((other, part))[0]
        part = dot(other, enc_weight[:, halves[k]]).astype(jnp.bfloat16)
        far[k] = lax.ppermute(part, "tok", SWAP)
    mine = lax.optimization_barrier((mine, part))[0]
    near[order[1]] = dot(mine, enc_weight[:, halves[order[1]]])
    for k in order:
        if codes:
            far[k] = lax.optimization_barrier((far[k], codes[order[0]]))[0]
        preact = near[k] + far[k].astype(jnp.float32) + enc_bias[None, halves[k]]
        codes[k] = jnp.maximum(preact, 0.0).astype(jnp.bfloat16)
    return codes[0], codes[1]


def lines_body(inputs, enc_weight, enc_bias, owner):
    batches, tok_rows, _ = inputs.shape
    tables = slot_tables(owner, batches * tok_rows * lax.axis_size("tok"))
    a, b = encode(inputs, enc_weight, enc_bias)
    return gather_and_tile(a, b, owner, *tables).transpose(1, 0, 2)


def select_blocks(codes_batch, picker):
    block_count = picker.shape[1]
    blocks = codes_batch.reshape(
        codes_batch.shape[0], block_count, codes_batch.shape[1] // block_count
    )
    chosen = jnp.einsum("sn,knt->skt", picker, blocks, preferred_element_type=jnp.float32)
    return chosen.astype(jnp.bfloat16)


def any_body(inputs, enc_weight, enc_bias, owner):
    batches, tok_rows, model_width = inputs.shape
    flat_rows = inputs.reshape(batches * tok_rows, model_width)
    preact = jnp.dot(
        flat_rows,
        lax.all_gather(enc_weight, "tok", axis=0, tiled=True),
        preferred_element_type=jnp.float32,
    )
    code_rows = jnp.maximum(preact + enc_bias[None, :], 0.0).astype(jnp.bfloat16)
    row_ids, col_ids, slot_scale = slot_tables(owner, batches * tok_rows * lax.axis_size("tok"))
    block_range = jnp.arange(F // TILE, dtype=jnp.int32)
    row_picker = (row_ids[:, None] == block_range[None, :]).astype(jnp.bfloat16)
    col_picker = (col_ids[:, None] == block_range[None, :]).astype(jnp.bfloat16)
    gathered = lax.all_gather(code_rows, "feat", axis=1, tiled=True)
    rows_blk = select_blocks(gathered, row_picker)
    cols_blk = select_blocks(gathered, col_picker)
    product = jnp.einsum("ska,skb->asb", rows_blk, cols_blk, preferred_element_type=jnp.float32)
    running = product * slot_scale[None, :, None]
    return lax.psum_scatter(running.astype(jnp.bfloat16), "tok", scatter_dimension=0, tiled=True)


def solution(mesh):
    in_specs = (P(None, ("groups", "tok"), None), P("tok", "feat"), P("feat"), P("feat"))
    out_specs = P("tok", ("groups", "feat"), None)
    lines = mesh.shape["feat"] == 8 and mesh.shape["tok"] == 2
    body = lines_body if lines else any_body
    return jax.shard_map(body, mesh=mesh, in_specs=in_specs, out_specs=out_specs, check_vma=False)
```

time: 191 us -> 174 us (0.911)
  Pallas kernels: 73.5 us -> 43.8 us
  waiting for transfers between devices: 62.9 us -> 90 us
  starting transfers between devices: 30.7 us -> 25.3 us
  local copies, waits for them, and re-layouts: 5.03 us -> 0.12 us
  other arithmetic: 7.92 us -> 4.37 us
    pallas_call x5, Pallas kernels: 73.5 us -> 43.8 us  [tiles(): pl.pallas_call(functools.partial(tiles_kernel, tuple(sources), len(pieces...]
    ppermute x32 -> x29, waiting for transfers between devices: 61 us -> 90 us  [send(): return lax.ppermute(array, axis, pairs)]
    ppermute x32 -> x29, starting transfers between devices: 29.5 us -> 24.1 us  [send(): return lax.ppermute(array, axis, pairs)]
    unnamed x66 -> x12, local copies, waits for them, and re-layouts: 4.36 us -> 0.03 us
    another operation x4 -> x0, other arithmetic: 2.41 us -> none  [work(): where = jnp.stack([half_at(me, key) for key in keys]).astype(jnp.int32)]
  transfers between devices with their start and end apart: 35 -> 32, of which waited for: 15 -> 17; matrix products, arithmetic and copies ran while one was open for 7% -> 5% of each run, Pallas kernels for 31% -> 21%
where the time goes in v2:
time: 174 us; the launch traced here: 173 us
  waiting for transfers between devices  90 us (52%)
  Pallas kernels  43.8 us (25%)
  starting transfers between devices  25.3 us (15%)
  matrix products  8.56 us (5%)
  other arithmetic  4.37 us (3%)
    ppermute x29, waiting for transfers between devices, send(): return lax.ppermute(array, axis, pairs)  90 us
    pallas_call x5, Pallas kernels, tiles(): pl.pallas_call(functools.partial(tiles_kernel, tuple(sources), len(pieces...  43.8 us
    ppermute x29, starting transfers between devices, send(): return lax.ppermute(array, axis, pairs)  24.1 us
    dot_general x1, matrix products, encode(): near[order[0]] = dot(mine, enc_weight[:, halves[order[0]]])  3.81 us
  transfers between devices with their start and end apart: 32, of which 17 were waited for; matrix products, arithmetic and copies ran while one was open for 5% of the time, Pallas kernels for 21%

profile of v2, /device:TPU:0, one launch (start us, length us, event | category | flops | bytes accessed | tf_op | source)
XLA Modules:
  0.0 172.6 jit_solution(3209437967115643494)
XLA Ops:
  0.0 2.1 %broadcast_select_fusion = (bf16[384,1792]{1,0:T(8,128)(2,1)S(1)}, bf16[384,1792]{1,0:T(8,128)(2,1)S(1)}) fusion(pred[]{:T(512)S(6)} %eq.252, bf16[384,3584]{1,0:T(8,128)(2,1)} %bitcast.22), kind=kLoop, calls=%fused_computation.13 | loop fusion | flops 1376256 | bytes 5505025 | tf_op jit(solution)/shard_map/jit(_where)/select_n | solution.py:348
  2.6 3.8 %fusion.6 = f32[384,1024]{1,0:T(8,128)S(1)} fusion(bf16[384,1792]{1,0:T(8,128)(2,1)S(1)} %get-tuple-element.47, bf16[1792,2048]{1,0:T(8,128)(2,1)} %param.7), kind=kOutput, calls=%fused_computation.6 | convolution fusion | flops 1409286144 | bytes 6619136 | tf_op jit(solution)/shard_map/dot_general | solution.py:355
  6.5 1.6 fusion.8
  8.2 1.6 fusion.11
  10.3 1.6 fusion
  12.6 4.0 %collective-permute-start.6 = (bf16[384,1024]{1,0:T(8,128)(2,1)S(1)}, bf16[384,1024]{1,0:T(8,128)(2,1)S(1)}, u32[]{:S(2)}, u32[]{:S(2)}) collective-permute-start(bf16[384,1024]{1,0:T(8,128)(2,1)S(1)} %maximum_convert_fusion.refs_8_), channel_id=1, source_target_pairs={{0,4},{1,5},{4,0},{5,1},{2,6},{3,7},{6,2},{7,3},{8,12},{9,13},{12,... | collective-permute-start | bytes 2359304 | tf_op jit(solution)/shard_map/ppermute | solution.py:250
  17.0 1.5 collective-permute-start.3
  18.5 1.6 collective-permute-start.5
  20.9 30.5 %collective-permute-done.6.refs_16_ = bf16[384,1024]{1,0:T(8,128)(2,1)S(1)} collective-permute-done((bf16[384,1024]{1,0:T(8,128)(2,1)S(1)}, bf16[384,1024]{1,0:T(8,128)(2,1)S(1)}, u32[]{:S(2)}, u32[]{:S(2)}) %collective-permute-start.6) | collective-permute-done | bytes 786464 | tf_op jit(solution)/shard_map/ppermute | solution.py:250
  51.6 1.7 collective-permute-done.5.refs_15_
  54.3 1.3 collective-permute-start.11
  55.6 1.3 collective-permute-start.13
  57.7 1.7 collective-permute-done.10.refs_13_
  59.4 8.2 %shard_map.64 = (bf16[67,256,512]{2,1,0:T(8,128)(2,1)}, bf16[32,2,384,512]{3,2,1,0:T(8,128)(2,1)}, s32[1]{0:T(128)}) custom-call(s32[16]{0:T(128)S(1)} %stack.67.refs_0_, s32[67]{0:T(128)S(1)} %select_reduce_fusion.2.refs_1_, s32[8]{0:T(128)S(1)} %convert_reduce_fusion.1.refs_2_, s32[67]{0:T(128)S(1)} %get-tuple-element.88.refs_3_, ...), custom_call_target="tpu_custom_call" | custom-call | flops 1000 | bytes 1000 | tf_op jit(solution)/shard_map/pallas_call | solution.py:176
  67.6 24.0 %collective-permute-done.9.refs_12_ = bf16[384,1024]{1,0:T(8,128)(2,1)S(1)} collective-permute-done((bf16[384,1024]{1,0:T(8,128)(2,1)S(1)}, bf16[384,1024]{1,0:T(8,128)(2,1)S(1)}, u32[]{:S(2)}, u32[]{:S(2)}) %collective-permute-start.9) | collective-permute-done | bytes 786464 | tf_op jit(solution)/shard_map/ppermute | solution.py:250
  91.6 2.3 %collective-permute-done.13 = bf16[384,1024]{1,0:T(8,128)(2,1)S(1)} collective-permute-done((bf16[384,1024]{1,0:T(8,128)(2,1)S(1)}, bf16[384,1024]{1,0:T(8,128)(2,1)S(1)}, u32[]{:S(2)}, u32[]{:S(2)}) %collective-permute-start.13) | collective-permute-done | bytes 786464 | tf_op jit(solution)/shard_map/ppermute | solution.py:250
  96.2 1.3 collective-permute-start.14
  98.4 9.6 %shard_map.65 = (bf16[67,256,512]{2,1,0:T(8,128)(2,1)}, bf16[32,2,384,512]{3,2,1,0:T(8,128)(2,1)}, s32[1]{0:T(128)}) custom-call(s32[16]{0:T(128)S(1)} %stack.67.refs_0_, s32[67]{0:T(128)S(1)} %select_reduce_fusion.2.refs_1_, s32[8]{0:T(128)S(1)} %convert_reduce_fusion.1.refs_2_, ...), custom_call_target="tpu_custom_call", output_to_operand_aliasing={{0}: (14, {}), {1}: (15, {})} | custom-call | flops 1000 | bytes 1000 | tf_op jit(solution)/shard_map/pallas_call | solution.py:176
  108.4 6.8 %collective-permute-done.18.refs_8_ = bf16[384,1024]{1,0:T(8,128)(2,1)S(1)} collective-permute-done((bf16[384,1024]{1,0:T(8,128)(2,1)S(1)}, bf16[384,1024]{1,0:T(8,128)(2,1)S(1)}, u32[]{:S(2)}, u32[]{:S(2)}) %collective-permute-start.18) | collective-permute-done | bytes 786464 | tf_op jit(solution)/shard_map/ppermute | solution.py:250
  115.1 2.6 %collective-permute-done.14 = bf16[384,1024]{1,0:T(8,128)(2,1)S(1)} collective-permute-done((bf16[384,1024]{1,0:T(8,128)(2,1)S(1)}, bf16[384,1024]{1,0:T(8,128)(2,1)S(1)}, u32[]{:S(2)}, u32[]{:S(2)}) %collective-permute-start.14) | collective-permute-done | bytes 786464 | tf_op jit(solution)/shard_map/ppermute | solution.py:250
  119.2 1.6 collective-permute-start.23
  120.7 2.6 %collective-permute-start.24 = (bf16[384,1024]{1,0:T(8,128)(2,1)S(1)}, bf16[384,1024]{1,0:T(8,128)(2,1)S(1)}, u32[]{:S(2)}, u32[]{:S(2)}) collective-permute-start(bf16[384,1024]{1,0:T(8,128)(2,1)S(1)} %maximum_convert_fusion.1.refs_10_), channel_id=1, source_target_pairs={{0,2},{1,3},{2,0},{3,1},{4,6},{5,7},{6,4},{7,5},{8,10},{9,11},{10,... | collective-permute-start | bytes 2359304 | tf_op jit(solution)/shard_map/ppermute | solution.py:250
  123.4 7.8 %shard_map.66 = (bf16[67,256,512]{2,1,0:T(8,128)(2,1)}, bf16[32,2,384,512]{3,2,1,0:T(8,128)(2,1)}, s32[1]{0:T(128)}) custom-call(s32[16]{0:T(128)S(1)} %stack.67.refs_0_, s32[67]{0:T(128)S(1)} %select_reduce_fusion.2.refs_1_, s32[8]{0:T(128)S(1)} %convert_reduce_fusion.1.refs_2_, ...), custom_call_target="tpu_custom_call", output_to_operand_aliasing={{0}: (12, {}), {1}: (13, {})} | custom-call | flops 1000 | bytes 1000 | tf_op jit(solution)/shard_map/pallas_call | solution.py:176
  131.5 7.2 %collective-permute-done.23.refs_8_ = bf16[384,1024]{1,0:T(8,128)(2,1)S(1)} collective-permute-done((bf16[384,1024]{1,0:T(8,128)(2,1)S(1)}, bf16[384,1024]{1,0:T(8,128)(2,1)S(1)}, u32[]{:S(2)}, u32[]{:S(2)}) %collective-permute-start.23) | collective-permute-done | bytes 786464 | tf_op jit(solution)/shard_map/ppermute | solution.py:250
  138.7 1.8 %collective-permute-done.24.refs_12_ = bf16[384,1024]{1,0:T(8,128)(2,1)S(1)} collective-permute-done((bf16[384,1024]{1,0:T(8,128)(2,1)S(1)}, bf16[384,1024]{1,0:T(8,128)(2,1)S(1)}, u32[]{:S(2)}, u32[]{:S(2)}) %collective-permute-start.24) | collective-permute-done | bytes 786464 | tf_op jit(solution)/shard_map/ppermute | solution.py:250
  141.9 1.7 %collective-permute-start.29 = (bf16[384,1024]{1,0:T(8,128)(2,1)S(1)}, bf16[384,1024]{1,0:T(8,128)(2,1)S(1)}, u32[]{:S(2)}, u32[]{:S(2)}) collective-permute-start(bf16[384,1024]{1,0:T(8,128)(2,1)S(1)} %collective-permute-done.4.refs_14_), channel_id=1, source_target_pairs={{0,2},{1,3},{2,0},{3,1},{4,6},{5,7},{6,4},{7,5},{8,10},{9,11},{10,... | collective-permute-start | bytes 2359304 | tf_op jit(solution)/shard_map/ppermute | solution.py:250
  143.9 1.1 collective-permute-done.28.refs_13_
  145.0 10.8 %shard_map.67 = (bf16[67,256,512]{2,1,0:T(8,128)(2,1)}, bf16[32,2,384,512]{3,2,1,0:T(8,128)(2,1)}, s32[1]{0:T(128)}) custom-call(s32[16]{0:T(128)S(1)} %stack.67.refs_0_, s32[67]{0:T(128)S(1)} %select_reduce_fusion.2.refs_1_, s32[8]{0:T(128)S(1)} %convert_reduce_fusion.1.refs_2_, ...), custom_call_target="tpu_custom_call", output_to_operand_aliasing={{0}: (14, {}), {1}: (15, {})} | custom-call | flops 1000 | bytes 1000 | tf_op jit(solution)/shard_map/pallas_call | solution.py:176
  155.8 5.2 %collective-permute-done.25.refs_8_ = bf16[384,1024]{1,0:T(8,128)(2,1)S(1)} collective-permute-done((bf16[384,1024]{1,0:T(8,128)(2,1)S(1)}, bf16[384,1024]{1,0:T(8,128)(2,1)S(1)}, u32[]{:S(2)}, u32[]{:S(2)}) %collective-permute-start.25) | collective-permute-done | bytes 786464 | tf_op jit(solution)/shard_map/ppermute | solution.py:250
  162.1 1.8 %collective-permute-done.30.refs_9_ = bf16[384,1024]{1,0:T(8,128)(2,1)S(1)} collective-permute-done((bf16[384,1024]{1,0:T(8,128)(2,1)S(1)}, bf16[384,1024]{1,0:T(8,128)(2,1)S(1)}, u32[]{:S(2)}, u32[]{:S(2)}) %collective-permute-start.30) | collective-permute-done | bytes 786464 | tf_op jit(solution)/shard_map/ppermute | solution.py:250
  163.9 1.1 collective-permute-done.31.refs_11_
  165.0 7.4 %shard_map.68 = (bf16[67,256,512]{2,1,0:T(8,128)(2,1)}, bf16[32,2,384,512]{3,2,1,0:T(8,128)(2,1)}, s32[1]{0:T(128)}) custom-call(s32[16]{0:T(128)S(1)} %stack.67.refs_0_, s32[67]{0:T(128)S(1)} %select_reduce_fusion.2.refs_1_, s32[8]{0:T(128)S(1)} %convert_reduce_fusion.1.refs_2_, ...), custom_call_target="tpu_custom_call", output_to_operand_aliasing={{0}: (12, {}), {1}: (13, {})} | custom-call | flops 1000 | bytes 1000 | tf_op jit(solution)/shard_map/pallas_call | solution.py:176
  (70 shorter events, 13.1 us)
Async XLA Ops:
  2.1 4.3 %collective-permute-start = (bf16[384,1792]{1,0:T(8,128)(2,1)S(1)}, bf16[384,1792]{1,0:T(8,128)(2,1)S(1)}, u32[]{:S(2)}, u32[]{:S(2)}) collective-permute-start(bf16[384,1792]{1,0:T(8,128)(2,1)S(1)} %get-tuple-element.91), channel_id=1, source_target_pairs={{0,8},{8,0},{1,9},{9,1},{2,10},{10,2},{3,11},{11,3},{4,12},{12,4},... | collective-permute-start | bytes 4128776 | tf_op jit(solution)/shard_map/ppermute | solution.py:349
  8.1 3.8 %collective-permute-start.1 = (bf16[384,1024]{1,0:T(8,128)(2,1)S(1)}, bf16[384,1024]{1,0:T(8,128)(2,1)S(1)}, u32[]{:S(2)}, u32[]{:S(2)}) collective-permute-start(bf16[384,1024]{1,0:T(8,128)(2,1)S(1)} %fusion.8), channel_id=1, source_target_pairs={{0,8},{8,0},{1,9},{9,1},{2,10},{10,2},{3,11},{11,3},{4,12},{12,4},... | collective-permute-start | bytes 2359304 | tf_op jit(solution)/shard_map/ppermute | solution.py:361
  9.8 2.5 %collective-permute-start.2 = (bf16[384,1024]{1,0:T(8,128)(2,1)S(1)}, bf16[384,1024]{1,0:T(8,128)(2,1)S(1)}, u32[]{:S(2)}, u32[]{:S(2)}) collective-permute-start(bf16[384,1024]{1,0:T(8,128)(2,1)S(1)} %fusion.11), channel_id=1, source_target_pairs={{0,8},{8,0},{1,9},{9,1},{2,10},{10,2},{3,11},{11,3},{4,12},{12,4},... | collective-permute-start | bytes 2359304 | tf_op jit(solution)/shard_map/ppermute | solution.py:361
  12.6 38.8 %collective-permute-start.6 = (bf16[384,1024]{1,0:T(8,128)(2,1)S(1)}, bf16[384,1024]{1,0:T(8,128)(2,1)S(1)}, u32[]{:S(2)}, u32[]{:S(2)}) collective-permute-start(bf16[384,1024]{1,0:T(8,128)(2,1)S(1)} %maximum_convert_fusion.refs_8_), channel_id=1, source_target_pairs={{0,4},{1,5},{4,0},{5,1},{2,6},{3,7},{6,2},{7,3},{8,12},{9,13},{12,... | collective-permute-start | bytes 2359304 | tf_op jit(solution)/shard_map/ppermute | solution.py:250
  17.0 34.6 %collective-permute-start.3 = (bf16[384,1024]{1,0:T(8,128)(2,1)S(1)}, bf16[384,1024]{1,0:T(8,128)(2,1)S(1)}, u32[]{:S(2)}, u32[]{:S(2)}) collective-permute-start(bf16[384,1024]{1,0:T(8,128)(2,1)S(1)} %maximum_convert_fusion.refs_8_), channel_id=1, source_target_pairs={{0,1},{1,0},{2,3},{3,2},{4,5},{5,4},{6,7},{7,6},{8,9},{9,8},{10,11... | collective-permute-start | bytes 2359304 | tf_op jit(solution)/shard_map/ppermute | solution.py:250
  18.5 34.8 %collective-permute-start.5 = (bf16[384,1024]{1,0:T(8,128)(2,1)S(1)}, bf16[384,1024]{1,0:T(8,128)(2,1)S(1)}, u32[]{:S(2)}, u32[]{:S(2)}) collective-permute-start(bf16[384,1024]{1,0:T(8,128)(2,1)S(1)} %maximum_convert_fusion.refs_8_), channel_id=1, source_target_pairs={{0,2},{1,3},{2,0},{3,1},{4,6},{5,7},{6,4},{7,5},{8,10},{9,11},{10,... | collective-permute-start | bytes 2359304 | tf_op jit(solution)/shard_map/ppermute | solution.py:250
  20.1 33.2 %collective-permute-start.4 = (bf16[384,1024]{1,0:T(8,128)(2,1)S(1)}, bf16[384,1024]{1,0:T(8,128)(2,1)S(1)}, u32[]{:S(2)}, u32[]{:S(2)}) collective-permute-start(bf16[384,1024]{1,0:T(8,128)(2,1)S(1)} %maximum_convert_fusion.1.refs_10_), channel_id=1, source_target_pairs={{0,1},{1,0},{2,3},{3,2},{4,5},{5,4},{6,7},{7,6},{8,9},{9,8},{10,11... | collective-permute-start | bytes 2359304 | tf_op jit(solution)/shard_map/ppermute | solution.py:250
  20.8 32.8 %collective-permute-start.7 = (bf16[384,1024]{1,0:T(8,128)(2,1)S(1)}, bf16[384,1024]{1,0:T(8,128)(2,1)S(1)}, u32[]{:S(2)}, u32[]{:S(2)}) collective-permute-start(bf16[384,1024]{1,0:T(8,128)(2,1)S(1)} %maximum_convert_fusion.refs_8_), channel_id=1, source_target_pairs={{0,8},{8,0},{1,9},{9,1},{2,10},{10,2},{3,11},{11,3},{4,12},{12,4},... | collective-permute-start | bytes 2359304 | tf_op jit(solution)/shard_map/ppermute | solution.py:250
  51.4 2.3 %collective-permute-start.8 = (bf16[384,1024]{1,0:T(8,128)(2,1)S(1)}, bf16[384,1024]{1,0:T(8,128)(2,1)S(1)}, u32[]{:S(2)}, u32[]{:S(2)}) collective-permute-start(bf16[384,1024]{1,0:T(8,128)(2,1)S(1)} %maximum_convert_fusion.1.refs_10_), channel_id=1, source_target_pairs={{0,8},{8,0},{1,9},{9,1},{2,10},{10,2},{3,11},{11,3},{4,12},{12,4},... | collective-permute-start | bytes 2359304 | tf_op jit(solution)/shard_map/ppermute | solution.py:250
  53.7 5.7 %collective-permute-start.10 = (bf16[1536,1024]{1,0:T(8,128)(2,1)S(1)}, bf16[1536,1024]{1,0:T(8,128)(2,1)S(1)}, u32[]{:S(2)}, u32[]{:S(2)}) collective-permute-start(bf16[1536,1024]{1,0:T(8,128)(2,1)S(1)} %pad_maximum_fusion), channel_id=1, source_target_pairs={{0,8},{8,0},{1,9},{9,1},{2,10},{10,2},{3,11},{11,3},{4,12},{12,4},... | collective-permute-start | bytes 9437192 | tf_op jit(solution)/shard_map/ppermute | solution.py:250
  53.8 37.8 %collective-permute-start.9 = (bf16[384,1024]{1,0:T(8,128)(2,1)S(1)}, bf16[384,1024]{1,0:T(8,128)(2,1)S(1)}, u32[]{:S(2)}, u32[]{:S(2)}) collective-permute-start(bf16[384,1024]{1,0:T(8,128)(2,1)S(1)} %maximum_convert_fusion.1.refs_10_), channel_id=1, source_target_pairs={{0,4},{1,5},{4,0},{5,1},{2,6},{3,7},{6,2},{7,3},{8,12},{9,13},{12,... | collective-permute-start | bytes 2359304 | tf_op jit(solution)/shard_map/ppermute | solution.py:250
  54.3 37.2 %collective-permute-start.11 = (bf16[384,1024]{1,0:T(8,128)(2,1)S(1)}, bf16[384,1024]{1,0:T(8,128)(2,1)S(1)}, u32[]{:S(2)}, u32[]{:S(2)}) collective-permute-start(bf16[384,1024]{1,0:T(8,128)(2,1)S(1)} %collective-permute-done.5.refs_15_), channel_id=1, source_target_pairs={{0,1},{1,0},{2,3},{3,2},{4,5},{5,4},{6,7},{7,6},{8,9},{9,8},{10,11... | collective-permute-start | bytes 2359304 | tf_op jit(solution)/shard_map/ppermute | solution.py:250
  55.6 38.3 %collective-permute-start.13 = (bf16[384,1024]{1,0:T(8,128)(2,1)S(1)}, bf16[384,1024]{1,0:T(8,128)(2,1)S(1)}, u32[]{:S(2)}, u32[]{:S(2)}) collective-permute-start(bf16[384,1024]{1,0:T(8,128)(2,1)S(1)} %collective-permute-done.6.refs_16_), channel_id=1, source_target_pairs={{2,0},{3,1},{4,6},{5,7},{10,8},{11,9},{12,14},{13,15},{18,16},{19,... | collective-permute-start | bytes 2359304 | tf_op jit(solution)/shard_map/ppermute | solution.py:250
  56.9 37.0 %collective-permute-start.12 = (bf16[384,1024]{1,0:T(8,128)(2,1)S(1)}, bf16[384,1024]{1,0:T(8,128)(2,1)S(1)}, u32[]{:S(2)}, u32[]{:S(2)}) collective-permute-start(bf16[384,1024]{1,0:T(8,128)(2,1)S(1)} %collective-permute-done.6.refs_16_), channel_id=1, source_target_pairs={{0,1},{1,0},{2,3},{3,2},{4,5},{5,4},{6,7},{7,6},{8,9},{9,8},{10,11... | collective-permute-start | bytes 2359304 | tf_op jit(solution)/shard_map/ppermute | solution.py:250
  93.9 2.3 %collective-permute-start.17 = (bf16[384,1024]{1,0:T(8,128)(2,1)S(1)}, bf16[384,1024]{1,0:T(8,128)(2,1)S(1)}, u32[]{:S(2)}, u32[]{:S(2)}) collective-permute-start(bf16[384,1024]{1,0:T(8,128)(2,1)S(1)} %collective-permute-done.9.refs_12_), channel_id=1, source_target_pairs={{0,8},{8,0},{1,9},{9,1},{2,10},{10,2},{3,11},{11,3},{4,12},{12,4},... | collective-permute-start | bytes 2359304 | tf_op jit(solution)/shard_map/ppermute | solution.py:250
  93.9 3.6 %collective-permute-start.15 = (bf16[384,1024]{1,0:T(8,128)(2,1)S(1)}, bf16[384,1024]{1,0:T(8,128)(2,1)S(1)}, u32[]{:S(2)}, u32[]{:S(2)}) collective-permute-start(bf16[384,1024]{1,0:T(8,128)(2,1)S(1)} %collective-permute-done.11.refs_8_), channel_id=1, source_target_pairs={{0,8},{8,0},{1,9},{9,1},{2,10},{10,2},{3,11},{11,3},{4,12},{12,4},... | collective-permute-start | bytes 2359304 | tf_op jit(solution)/shard_map/ppermute | solution.py:250
  94.4 4.0 %collective-permute-start.16 = (bf16[384,1024]{1,0:T(8,128)(2,1)S(1)}, bf16[384,1024]{1,0:T(8,128)(2,1)S(1)}, u32[]{:S(2)}, u32[]{:S(2)}) collective-permute-start(bf16[384,1024]{1,0:T(8,128)(2,1)S(1)} %collective-permute-done.12.refs_10_), channel_id=1, source_target_pairs={{0,8},{8,0},{1,9},{9,1},{2,10},{10,2},{3,11},{11,3},{4,12},{12,4},... | collective-permute-start | bytes 2359304 | tf_op jit(solution)/shard_map/ppermute | solution.py:250
  94.4 13.6 %collective-permute-start.19 = (bf16[384,1024]{1,0:T(8,128)(2,1)S(1)}, bf16[384,1024]{1,0:T(8,128)(2,1)S(1)}, u32[]{:S(2)}, u32[]{:S(2)}) collective-permute-start(bf16[384,1024]{1,0:T(8,128)(2,1)S(1)} %maximum_convert_fusion.refs_8_), channel_id=1, source_target_pairs={{2,4},{3,5},{4,2},{5,3},{10,12},{11,13},{12,10},{13,11},{18,20},{1... | collective-permute-start | bytes 2359304 | tf_op jit(solution)/shard_map/ppermute | solution.py:250
  95.1 20.0 %collective-permute-start.18 = (bf16[384,1024]{1,0:T(8,128)(2,1)S(1)}, bf16[384,1024]{1,0:T(8,128)(2,1)S(1)}, u32[]{:S(2)}, u32[]{:S(2)}) collective-permute-start(bf16[384,1024]{1,0:T(8,128)(2,1)S(1)} %collective-permute-done.9.refs_12_), channel_id=1, source_target_pairs={{0,1},{1,0},{2,3},{3,2},{4,5},{5,4},{6,7},{7,6},{8,9},{9,8},{10,11... | collective-permute-start | bytes 2359304 | tf_op jit(solution)/shard_map/ppermute | solution.py:250
  96.2 21.6 %collective-permute-start.14 = (bf16[384,1024]{1,0:T(8,128)(2,1)S(1)}, bf16[384,1024]{1,0:T(8,128)(2,1)S(1)}, u32[]{:S(2)}, u32[]{:S(2)}) collective-permute-start(bf16[384,1024]{1,0:T(8,128)(2,1)S(1)} %collective-permute-done.9.refs_12_), channel_id=1, source_target_pairs={{2,0},{3,1},{4,6},{5,7},{10,8},{11,9},{12,14},{13,15},{18,16},{19,... | collective-permute-start | bytes 2359304 | tf_op jit(solution)/shard_map/ppermute | solution.py:250
  117.8 5.6 %collective-permute-start.22 = (bf16[384,1024]{1,0:T(8,128)(2,1)S(1)}, bf16[384,1024]{1,0:T(8,128)(2,1)S(1)}, u32[]{:S(2)}, u32[]{:S(2)}) collective-permute-start(bf16[384,1024]{1,0:T(8,128)(2,1)S(1)} %add.209.refs_10_), channel_id=1, source_target_pairs={{0,8},{8,0},{1,9},{9,1},{2,10},{10,2},{3,11},{11,3},{4,12},{12,4},... | collective-permute-start | bytes 2359304 | tf_op jit(solution)/shard_map/ppermute | solution.py:250
  117.8 5.6 %collective-permute-start.21 = (bf16[384,1024]{1,0:T(8,128)(2,1)S(1)}, bf16[384,1024]{1,0:T(8,128)(2,1)S(1)}, u32[]{:S(2)}, u32[]{:S(2)}) collective-permute-start(bf16[384,1024]{1,0:T(8,128)(2,1)S(1)} %collective-permute-done.18.refs_8_), channel_id=1, source_target_pairs={{0,8},{8,0},{1,9},{9,1},{2,10},{10,2},{3,11},{11,3},{4,12},{12,4},... | collective-permute-start | bytes 2359304 | tf_op jit(solution)/shard_map/ppermute | solution.py:250
  118.3 12.9 %collective-permute-start.20 = (bf16[384,1024]{1,0:T(8,128)(2,1)S(1)}, bf16[384,1024]{1,0:T(8,128)(2,1)S(1)}, u32[]{:S(2)}, u32[]{:S(2)}) collective-permute-start(bf16[384,1024]{1,0:T(8,128)(2,1)S(1)} %maximum_convert_fusion.1.refs_10_), channel_id=1, source_target_pairs={{2,4},{3,5},{4,2},{5,3},{10,12},{11,13},{12,10},{13,11},{18,20},{1... | collective-permute-start | bytes 2359304 | tf_op jit(solution)/shard_map/ppermute | solution.py:250
  119.2 19.5 %collective-permute-start.23 = (bf16[384,1024]{1,0:T(8,128)(2,1)S(1)}, bf16[384,1024]{1,0:T(8,128)(2,1)S(1)}, u32[]{:S(2)}, u32[]{:S(2)}) collective-permute-start(bf16[384,1024]{1,0:T(8,128)(2,1)S(1)} %add.209.refs_10_), channel_id=1, source_target_pairs={{0,1},{1,0},{2,3},{3,2},{4,5},{5,4},{6,7},{7,6},{8,9},{9,8},{10,11... | collective-permute-start | bytes 2359304 | tf_op jit(solution)/shard_map/ppermute | solution.py:250
  120.7 19.8 %collective-permute-start.24 = (bf16[384,1024]{1,0:T(8,128)(2,1)S(1)}, bf16[384,1024]{1,0:T(8,128)(2,1)S(1)}, u32[]{:S(2)}, u32[]{:S(2)}) collective-permute-start(bf16[384,1024]{1,0:T(8,128)(2,1)S(1)} %maximum_convert_fusion.1.refs_10_), channel_id=1, source_target_pairs={{0,2},{1,3},{2,0},{3,1},{4,6},{5,7},{6,4},{7,5},{8,10},{9,11},{10,... | collective-permute-start | bytes 2359304 | tf_op jit(solution)/shard_map/ppermute | solution.py:250
  140.5 3.2 %collective-permute-start.27 = (bf16[384,1024]{1,0:T(8,128)(2,1)S(1)}, bf16[384,1024]{1,0:T(8,128)(2,1)S(1)}, u32[]{:S(2)}, u32[]{:S(2)}) collective-permute-start(bf16[384,1024]{1,0:T(8,128)(2,1)S(1)} %add.208.refs_10_), channel_id=1, source_target_pairs={{0,8},{8,0},{1,9},{9,1},{2,10},{10,2},{3,11},{11,3},{4,12},{12,4},... | collective-permute-start | bytes 2359304 | tf_op jit(solution)/shard_map/ppermute | solution.py:250
  140.5 3.4 %collective-permute-start.26 = (bf16[384,1024]{1,0:T(8,128)(2,1)S(1)}, bf16[384,1024]{1,0:T(8,128)(2,1)S(1)}, u32[]{:S(2)}, u32[]{:S(2)}) collective-permute-start(bf16[384,1024]{1,0:T(8,128)(2,1)S(1)} %collective-permute-done.23.refs_8_), channel_id=1, source_target_pairs={{0,8},{8,0},{1,9},{9,1},{2,10},{10,2},{3,11},{11,3},{4,12},{12,4},... | collective-permute-start | bytes 2359304 | tf_op jit(solution)/shard_map/ppermute | solution.py:250
  141.0 4.0 %collective-permute-start.28 = (bf16[384,1024]{1,0:T(8,128)(2,1)S(1)}, bf16[384,1024]{1,0:T(8,128)(2,1)S(1)}, u32[]{:S(2)}, u32[]{:S(2)}) collective-permute-start(bf16[384,1024]{1,0:T(8,128)(2,1)S(1)} %collective-permute-done.24.refs_12_), channel_id=1, source_target_pairs={{0,8},{8,0},{1,9},{9,1},{2,10},{10,2},{3,11},{11,3},{4,12},{12,4},... | collective-permute-start | bytes 2359304 | tf_op jit(solution)/shard_map/ppermute | solution.py:250
  141.0 20.0 %collective-permute-start.25 = (bf16[384,1024]{1,0:T(8,128)(2,1)S(1)}, bf16[384,1024]{1,0:T(8,128)(2,1)S(1)}, u32[]{:S(2)}, u32[]{:S(2)}) collective-permute-start(bf16[384,1024]{1,0:T(8,128)(2,1)S(1)} %add.208.refs_10_), channel_id=1, source_target_pairs={{0,1},{1,0},{2,3},{3,2},{4,5},{5,4},{6,7},{7,6},{8,9},{9,8},{10,11... | collective-permute-start | bytes 2359304 | tf_op jit(solution)/shard_map/ppermute | solution.py:250
  141.9 19.7 %collective-permute-start.29 = (bf16[384,1024]{1,0:T(8,128)(2,1)S(1)}, bf16[384,1024]{1,0:T(8,128)(2,1)S(1)}, u32[]{:S(2)}, u32[]{:S(2)}) collective-permute-start(bf16[384,1024]{1,0:T(8,128)(2,1)S(1)} %collective-permute-done.4.refs_14_), channel_id=1, source_target_pairs={{0,2},{1,3},{2,0},{3,1},{4,6},{5,7},{6,4},{7,5},{8,10},{9,11},{10,... | collective-permute-start | bytes 2359304 | tf_op jit(solution)/shard_map/ppermute | solution.py:250
  161.6 2.3 %collective-permute-start.30 = (bf16[384,1024]{1,0:T(8,128)(2,1)S(1)}, bf16[384,1024]{1,0:T(8,128)(2,1)S(1)}, u32[]{:S(2)}, u32[]{:S(2)}) collective-permute-start(bf16[384,1024]{1,0:T(8,128)(2,1)S(1)} %collective-permute-done.25.refs_8_), channel_id=1, source_target_pairs={{0,8},{8,0},{1,9},{9,1},{2,10},{10,2},{3,11},{11,3},{4,12},{12,4},... | collective-permute-start | bytes 2359304 | tf_op jit(solution)/shard_map/ppermute | solution.py:250
  161.6 3.4 %collective-permute-start.31 = (bf16[384,1024]{1,0:T(8,128)(2,1)S(1)}, bf16[384,1024]{1,0:T(8,128)(2,1)S(1)}, u32[]{:S(2)}, u32[]{:S(2)}) collective-permute-start(bf16[384,1024]{1,0:T(8,128)(2,1)S(1)} %collective-permute-done.29.refs_10_), channel_id=1, source_target_pairs={{0,8},{8,0},{1,9},{9,1},{2,10},{10,2},{3,11},{11,3},{4,12},{12,4},... | collective-permute-start | bytes 2359304 | tf_op jit(solution)/shard_map/ppermute | solution.py:250
  (6 other events, 27.2 us)

commit v3 on v2

--- a/solution.py
+++ b/solution.py
@@ -333,7 +333,6 @@
     m.keep(p101=n1b)
     state = work(3, state)
 
-    m.after(x3b, x1b)
     m.keep(p311=x3b)
     m.keep(p111=x1b)
     return work(4, state)[0]

time: 174 us -> 174 us (level)
  no operation moved by 1% of the time
where the time goes in v3:
time: 174 us; the launch traced here: 173 us
  waiting for transfers between devices  89.8 us (52%)
  Pallas kernels  45.1 us (26%)
  starting transfers between devices  24.9 us (14%)
  matrix products  8.56 us (5%)
  other arithmetic  4.37 us (3%)
    ppermute x29, waiting for transfers between devices, send(): return lax.ppermute(array, axis, pairs)  89.7 us
    pallas_call x5, Pallas kernels, tiles(): pl.pallas_call(functools.partial(tiles_kernel, tuple(sources), len(pieces...  45.1 us
    ppermute x29, starting transfers between devices, send(): return lax.ppermute(array, axis, pairs)  23.7 us
    dot_general x1, matrix products, encode(): near[order[0]] = dot(mine, enc_weight[:, halves[order[0]]])  3.81 us
  transfers between devices with their start and end apart: 32, of which 17 were waited for; matrix products, arithmetic and copies ran while one was open for 5% of the time, Pallas kernels for 21%

profile of v3, /device:TPU:0, one launch (start us, length us, event | category | flops | bytes accessed | tf_op | source)
XLA Modules:
  0.0 173.4 jit_solution(10151580043749818161)
XLA Ops:
  0.0 2.1 %broadcast_select_fusion = (bf16[384,1792]{1,0:T(8,128)(2,1)S(1)}, bf16[384,1792]{1,0:T(8,128)(2,1)S(1)}) fusion(pred[]{:T(512)S(6)} %eq.252, bf16[384,3584]{1,0:T(8,128)(2,1)} %bitcast.22), kind=kLoop, calls=%fused_computation.13 | loop fusion | flops 1376256 | bytes 5505025 | tf_op jit(solution)/shard_map/jit(_where)/select_n | solution.py:347
  2.6 3.8 %fusion.6 = f32[384,1024]{1,0:T(8,128)S(1)} fusion(bf16[384,1792]{1,0:T(8,128)(2,1)S(1)} %get-tuple-element.47, bf16[1792,2048]{1,0:T(8,128)(2,1)} %param.7), kind=kOutput, calls=%fused_computation.6 | convolution fusion | flops 1409286144 | bytes 6619136 | tf_op jit(solution)/shard_map/dot_general | solution.py:354
  6.5 1.6 fusion.8
  8.2 1.6 fusion.11
  10.3 1.6 fusion
  12.6 4.0 %collective-permute-start.6 = (bf16[384,1024]{1,0:T(8,128)(2,1)S(1)}, bf16[384,1024]{1,0:T(8,128)(2,1)S(1)}, u32[]{:S(2)}, u32[]{:S(2)}) collective-permute-start(bf16[384,1024]{1,0:T(8,128)(2,1)S(1)} %maximum_convert_fusion.refs_8_), channel_id=1, source_target_pairs={{0,4},{1,5},{4,0},{5,1},{2,6},{3,7},{6,2},{7,3},{8,12},{9,13},{12,... | collective-permute-start | bytes 2359304 | tf_op jit(solution)/shard_map/ppermute | solution.py:250
  17.0 1.5 collective-permute-start.3
  18.5 1.6 collective-permute-start.5
  20.9 30.5 %collective-permute-done.6.refs_16_ = bf16[384,1024]{1,0:T(8,128)(2,1)S(1)} collective-permute-done((bf16[384,1024]{1,0:T(8,128)(2,1)S(1)}, bf16[384,1024]{1,0:T(8,128)(2,1)S(1)}, u32[]{:S(2)}, u32[]{:S(2)}) %collective-permute-start.6) | collective-permute-done | bytes 786464 | tf_op jit(solution)/shard_map/ppermute | solution.py:250
  51.6 1.7 collective-permute-done.5.refs_15_
  54.3 1.3 collective-permute-start.11
  55.6 1.3 collective-permute-start.13
  57.7 1.7 collective-permute-done.10.refs_13_
  59.4 8.3 %shard_map.64 = (bf16[67,256,512]{2,1,0:T(8,128)(2,1)}, bf16[32,2,384,512]{3,2,1,0:T(8,128)(2,1)}, s32[1]{0:T(128)}) custom-call(s32[16]{0:T(128)S(1)} %stack.67.refs_0_, s32[67]{0:T(128)S(1)} %select_reduce_fusion.2.refs_1_, s32[8]{0:T(128)S(1)} %convert_reduce_fusion.1.refs_2_, s32[67]{0:T(128)S(1)} %get-tuple-element.88.refs_3_, ...), custom_call_target="tpu_custom_call" | custom-call | flops 1000 | bytes 1000 | tf_op jit(solution)/shard_map/pallas_call | solution.py:176
  67.7 23.9 %collective-permute-done.9.refs_12_ = bf16[384,1024]{1,0:T(8,128)(2,1)S(1)} collective-permute-done((bf16[384,1024]{1,0:T(8,128)(2,1)S(1)}, bf16[384,1024]{1,0:T(8,128)(2,1)S(1)}, u32[]{:S(2)}, u32[]{:S(2)}) %collective-permute-start.9) | collective-permute-done | bytes 786464 | tf_op jit(solution)/shard_map/ppermute | solution.py:250
  91.6 2.3 %collective-permute-done.13 = bf16[384,1024]{1,0:T(8,128)(2,1)S(1)} collective-permute-done((bf16[384,1024]{1,0:T(8,128)(2,1)S(1)}, bf16[384,1024]{1,0:T(8,128)(2,1)S(1)}, u32[]{:S(2)}, u32[]{:S(2)}) %collective-permute-start.13) | collective-permute-done | bytes 786464 | tf_op jit(solution)/shard_map/ppermute | solution.py:250
  96.2 1.3 collective-permute-start.14
  98.4 8.6 %shard_map.65 = (bf16[67,256,512]{2,1,0:T(8,128)(2,1)}, bf16[32,2,384,512]{3,2,1,0:T(8,128)(2,1)}, s32[1]{0:T(128)}) custom-call(s32[16]{0:T(128)S(1)} %stack.67.refs_0_, s32[67]{0:T(128)S(1)} %select_reduce_fusion.2.refs_1_, s32[8]{0:T(128)S(1)} %convert_reduce_fusion.1.refs_2_, ...), custom_call_target="tpu_custom_call", output_to_operand_aliasing={{0}: (14, {}), {1}: (15, {})} | custom-call | flops 1000 | bytes 1000 | tf_op jit(solution)/shard_map/pallas_call | solution.py:176
  107.3 7.8 %collective-permute-done.18.refs_8_ = bf16[384,1024]{1,0:T(8,128)(2,1)S(1)} collective-permute-done((bf16[384,1024]{1,0:T(8,128)(2,1)S(1)}, bf16[384,1024]{1,0:T(8,128)(2,1)S(1)}, u32[]{:S(2)}, u32[]{:S(2)}) %collective-permute-start.18) | collective-permute-done | bytes 786464 | tf_op jit(solution)/shard_map/ppermute | solution.py:250
  115.1 2.6 %collective-permute-done.14 = bf16[384,1024]{1,0:T(8,128)(2,1)S(1)} collective-permute-done((bf16[384,1024]{1,0:T(8,128)(2,1)S(1)}, bf16[384,1024]{1,0:T(8,128)(2,1)S(1)}, u32[]{:S(2)}, u32[]{:S(2)}) %collective-permute-start.14) | collective-permute-done | bytes 786464 | tf_op jit(solution)/shard_map/ppermute | solution.py:250
  118.3 1.5 collective-permute-start.23
  120.7 2.7 %collective-permute-start.24 = (bf16[384,1024]{1,0:T(8,128)(2,1)S(1)}, bf16[384,1024]{1,0:T(8,128)(2,1)S(1)}, u32[]{:S(2)}, u32[]{:S(2)}) collective-permute-start(bf16[384,1024]{1,0:T(8,128)(2,1)S(1)} %maximum_convert_fusion.1.refs_10_), channel_id=1, source_target_pairs={{0,2},{1,3},{2,0},{3,1},{4,6},{5,7},{6,4},{7,5},{8,10},{9,11},{10,... | collective-permute-start | bytes 2359304 | tf_op jit(solution)/shard_map/ppermute | solution.py:250
  123.4 8.9 %shard_map.66 = (bf16[67,256,512]{2,1,0:T(8,128)(2,1)}, bf16[32,2,384,512]{3,2,1,0:T(8,128)(2,1)}, s32[1]{0:T(128)}) custom-call(s32[16]{0:T(128)S(1)} %stack.67.refs_0_, s32[67]{0:T(128)S(1)} %select_reduce_fusion.2.refs_1_, s32[8]{0:T(128)S(1)} %convert_reduce_fusion.1.refs_2_, ...), custom_call_target="tpu_custom_call", output_to_operand_aliasing={{0}: (12, {}), {1}: (13, {})} | custom-call | flops 1000 | bytes 1000 | tf_op jit(solution)/shard_map/pallas_call | solution.py:176
  132.3 5.4 %collective-permute-done.23.refs_8_ = bf16[384,1024]{1,0:T(8,128)(2,1)S(1)} collective-permute-done((bf16[384,1024]{1,0:T(8,128)(2,1)S(1)}, bf16[384,1024]{1,0:T(8,128)(2,1)S(1)}, u32[]{:S(2)}, u32[]{:S(2)}) %collective-permute-start.23) | collective-permute-done | bytes 786464 | tf_op jit(solution)/shard_map/ppermute | solution.py:250
  137.7 2.8 %collective-permute-done.24.refs_12_ = bf16[384,1024]{1,0:T(8,128)(2,1)S(1)} collective-permute-done((bf16[384,1024]{1,0:T(8,128)(2,1)S(1)}, bf16[384,1024]{1,0:T(8,128)(2,1)S(1)}, u32[]{:S(2)}, u32[]{:S(2)}) %collective-permute-start.24) | collective-permute-done | bytes 786464 | tf_op jit(solution)/shard_map/ppermute | solution.py:250
  142.4 1.7 %collective-permute-start.30 = (bf16[384,1024]{1,0:T(8,128)(2,1)S(1)}, bf16[384,1024]{1,0:T(8,128)(2,1)S(1)}, u32[]{:S(2)}, u32[]{:S(2)}) collective-permute-start(bf16[384,1024]{1,0:T(8,128)(2,1)S(1)} %collective-permute-done.4.refs_14_), channel_id=1, source_target_pairs={{0,2},{1,3},{2,0},{3,1},{4,6},{5,7},{6,4},{7,5},{8,10},{9,11},{10,... | collective-permute-start | bytes 2359304 | tf_op jit(solution)/shard_map/ppermute | solution.py:250
  144.3 1.1 collective-permute-done.28.refs_13_
  145.4 10.9 %shard_map.67 = (bf16[67,256,512]{2,1,0:T(8,128)(2,1)}, bf16[32,2,384,512]{3,2,1,0:T(8,128)(2,1)}, s32[1]{0:T(128)}) custom-call(s32[16]{0:T(128)S(1)} %stack.67.refs_0_, s32[67]{0:T(128)S(1)} %select_reduce_fusion.2.refs_1_, s32[8]{0:T(128)S(1)} %convert_reduce_fusion.1.refs_2_, ...), custom_call_target="tpu_custom_call", output_to_operand_aliasing={{0}: (14, {}), {1}: (15, {})} | custom-call | flops 1000 | bytes 1000 | tf_op jit(solution)/shard_map/pallas_call | solution.py:176
  156.4 5.0 %collective-permute-done.25.refs_8_ = bf16[384,1024]{1,0:T(8,128)(2,1)S(1)} collective-permute-done((bf16[384,1024]{1,0:T(8,128)(2,1)S(1)}, bf16[384,1024]{1,0:T(8,128)(2,1)S(1)}, u32[]{:S(2)}, u32[]{:S(2)}) %collective-permute-start.25) | collective-permute-done | bytes 786464 | tf_op jit(solution)/shard_map/ppermute | solution.py:250
  162.0 1.7 collective-permute-done.29.refs_9_
  163.7 1.1 collective-permute-done.31.refs_11_
  164.8 8.4 %shard_map.68 = (bf16[67,256,512]{2,1,0:T(8,128)(2,1)}, bf16[32,2,384,512]{3,2,1,0:T(8,128)(2,1)}, s32[1]{0:T(128)}) custom-call(s32[16]{0:T(128)S(1)} %stack.67.refs_0_, s32[67]{0:T(128)S(1)} %select_reduce_fusion.2.refs_1_, s32[8]{0:T(128)S(1)} %convert_reduce_fusion.1.refs_2_, ...), custom_call_target="tpu_custom_call", output_to_operand_aliasing={{0}: (12, {}), {1}: (13, {})} | custom-call | flops 1000 | bytes 1000 | tf_op jit(solution)/shard_map/pallas_call | solution.py:176
  (70 shorter events, 12.7 us)
Async XLA Ops:
  2.1 4.3 %collective-permute-start = (bf16[384,1792]{1,0:T(8,128)(2,1)S(1)}, bf16[384,1792]{1,0:T(8,128)(2,1)S(1)}, u32[]{:S(2)}, u32[]{:S(2)}) collective-permute-start(bf16[384,1792]{1,0:T(8,128)(2,1)S(1)} %get-tuple-element.91), channel_id=1, source_target_pairs={{0,8},{8,0},{1,9},{9,1},{2,10},{10,2},{3,11},{11,3},{4,12},{12,4},... | collective-permute-start | bytes 4128776 | tf_op jit(solution)/shard_map/ppermute | solution.py:348
  8.1 3.8 %collective-permute-start.1 = (bf16[384,1024]{1,0:T(8,128)(2,1)S(1)}, bf16[384,1024]{1,0:T(8,128)(2,1)S(1)}, u32[]{:S(2)}, u32[]{:S(2)}) collective-permute-start(bf16[384,1024]{1,0:T(8,128)(2,1)S(1)} %fusion.8), channel_id=1, source_target_pairs={{0,8},{8,0},{1,9},{9,1},{2,10},{10,2},{3,11},{11,3},{4,12},{12,4},... | collective-permute-start | bytes 2359304 | tf_op jit(solution)/shard_map/ppermute | solution.py:360
  9.8 2.5 %collective-permute-start.2 = (bf16[384,1024]{1,0:T(8,128)(2,1)S(1)}, bf16[384,1024]{1,0:T(8,128)(2,1)S(1)}, u32[]{:S(2)}, u32[]{:S(2)}) collective-permute-start(bf16[384,1024]{1,0:T(8,128)(2,1)S(1)} %fusion.11), channel_id=1, source_target_pairs={{0,8},{8,0},{1,9},{9,1},{2,10},{10,2},{3,11},{11,3},{4,12},{12,4},... | collective-permute-start | bytes 2359304 | tf_op jit(solution)/shard_map/ppermute | solution.py:360
  12.6 38.8 %collective-permute-start.6 = (bf16[384,1024]{1,0:T(8,128)(2,1)S(1)}, bf16[384,1024]{1,0:T(8,128)(2,1)S(1)}, u32[]{:S(2)}, u32[]{:S(2)}) collective-permute-start(bf16[384,1024]{1,0:T(8,128)(2,1)S(1)} %maximum_convert_fusion.refs_8_), channel_id=1, source_target_pairs={{0,4},{1,5},{4,0},{5,1},{2,6},{3,7},{6,2},{7,3},{8,12},{9,13},{12,... | collective-permute-start | bytes 2359304 | tf_op jit(solution)/shard_map/ppermute | solution.py:250
  17.0 34.6 %collective-permute-start.3 = (bf16[384,1024]{1,0:T(8,128)(2,1)S(1)}, bf16[384,1024]{1,0:T(8,128)(2,1)S(1)}, u32[]{:S(2)}, u32[]{:S(2)}) collective-permute-start(bf16[384,1024]{1,0:T(8,128)(2,1)S(1)} %maximum_convert_fusion.refs_8_), channel_id=1, source_target_pairs={{0,1},{1,0},{2,3},{3,2},{4,5},{5,4},{6,7},{7,6},{8,9},{9,8},{10,11... | collective-permute-start | bytes 2359304 | tf_op jit(solution)/shard_map/ppermute | solution.py:250
  18.5 34.8 %collective-permute-start.5 = (bf16[384,1024]{1,0:T(8,128)(2,1)S(1)}, bf16[384,1024]{1,0:T(8,128)(2,1)S(1)}, u32[]{:S(2)}, u32[]{:S(2)}) collective-permute-start(bf16[384,1024]{1,0:T(8,128)(2,1)S(1)} %maximum_convert_fusion.refs_8_), channel_id=1, source_target_pairs={{0,2},{1,3},{2,0},{3,1},{4,6},{5,7},{6,4},{7,5},{8,10},{9,11},{10,... | collective-permute-start | bytes 2359304 | tf_op jit(solution)/shard_map/ppermute | solution.py:250
  20.1 33.2 %collective-permute-start.4 = (bf16[384,1024]{1,0:T(8,128)(2,1)S(1)}, bf16[384,1024]{1,0:T(8,128)(2,1)S(1)}, u32[]{:S(2)}, u32[]{:S(2)}) collective-permute-start(bf16[384,1024]{1,0:T(8,128)(2,1)S(1)} %maximum_convert_fusion.1.refs_10_), channel_id=1, source_target_pairs={{0,1},{1,0},{2,3},{3,2},{4,5},{5,4},{6,7},{7,6},{8,9},{9,8},{10,11... | collective-permute-start | bytes 2359304 | tf_op jit(solution)/shard_map/ppermute | solution.py:250
  20.8 32.8 %collective-permute-start.7 = (bf16[384,1024]{1,0:T(8,128)(2,1)S(1)}, bf16[384,1024]{1,0:T(8,128)(2,1)S(1)}, u32[]{:S(2)}, u32[]{:S(2)}) collective-permute-start(bf16[384,1024]{1,0:T(8,128)(2,1)S(1)} %maximum_convert_fusion.refs_8_), channel_id=1, source_target_pairs={{0,8},{8,0},{1,9},{9,1},{2,10},{10,2},{3,11},{11,3},{4,12},{12,4},... | collective-permute-start | bytes 2359304 | tf_op jit(solution)/shard_map/ppermute | solution.py:250
  51.4 2.3 %collective-permute-start.8 = (bf16[384,1024]{1,0:T(8,128)(2,1)S(1)}, bf16[384,1024]{1,0:T(8,128)(2,1)S(1)}, u32[]{:S(2)}, u32[]{:S(2)}) collective-permute-start(bf16[384,1024]{1,0:T(8,128)(2,1)S(1)} %maximum_convert_fusion.1.refs_10_), channel_id=1, source_target_pairs={{0,8},{8,0},{1,9},{9,1},{2,10},{10,2},{3,11},{11,3},{4,12},{12,4},... | collective-permute-start | bytes 2359304 | tf_op jit(solution)/shard_map/ppermute | solution.py:250
  53.7 5.7 %collective-permute-start.10 = (bf16[1536,1024]{1,0:T(8,128)(2,1)S(1)}, bf16[1536,1024]{1,0:T(8,128)(2,1)S(1)}, u32[]{:S(2)}, u32[]{:S(2)}) collective-permute-start(bf16[1536,1024]{1,0:T(8,128)(2,1)S(1)} %pad_maximum_fusion), channel_id=1, source_target_pairs={{0,8},{8,0},{1,9},{9,1},{2,10},{10,2},{3,11},{11,3},{4,12},{12,4},... | collective-permute-start | bytes 9437192 | tf_op jit(solution)/shard_map/ppermute | solution.py:250
  53.8 37.8 %collective-permute-start.9 = (bf16[384,1024]{1,0:T(8,128)(2,1)S(1)}, bf16[384,1024]{1,0:T(8,128)(2,1)S(1)}, u32[]{:S(2)}, u32[]{:S(2)}) collective-permute-start(bf16[384,1024]{1,0:T(8,128)(2,1)S(1)} %maximum_convert_fusion.1.refs_10_), channel_id=1, source_target_pairs={{0,4},{1,5},{4,0},{5,1},{2,6},{3,7},{6,2},{7,3},{8,12},{9,13},{12,... | collective-permute-start | bytes 2359304 | tf_op jit(solution)/shard_map/ppermute | solution.py:250
  54.3 37.2 %collective-permute-start.11 = (bf16[384,1024]{1,0:T(8,128)(2,1)S(1)}, bf16[384,1024]{1,0:T(8,128)(2,1)S(1)}, u32[]{:S(2)}, u32[]{:S(2)}) collective-permute-start(bf16[384,1024]{1,0:T(8,128)(2,1)S(1)} %collective-permute-done.5.refs_15_), channel_id=1, source_target_pairs={{0,1},{1,0},{2,3},{3,2},{4,5},{5,4},{6,7},{7,6},{8,9},{9,8},{10,11... | collective-permute-start | bytes 2359304 | tf_op jit(solution)/shard_map/ppermute | solution.py:250
  55.6 38.3 %collective-permute-start.13 = (bf16[384,1024]{1,0:T(8,128)(2,1)S(1)}, bf16[384,1024]{1,0:T(8,128)(2,1)S(1)}, u32[]{:S(2)}, u32[]{:S(2)}) collective-permute-start(bf16[384,1024]{1,0:T(8,128)(2,1)S(1)} %collective-permute-done.6.refs_16_), channel_id=1, source_target_pairs={{2,0},{3,1},{4,6},{5,7},{10,8},{11,9},{12,14},{13,15},{18,16},{19,... | collective-permute-start | bytes 2359304 | tf_op jit(solution)/shard_map/ppermute | solution.py:250
  56.9 37.0 %collective-permute-start.12 = (bf16[384,1024]{1,0:T(8,128)(2,1)S(1)}, bf16[384,1024]{1,0:T(8,128)(2,1)S(1)}, u32[]{:S(2)}, u32[]{:S(2)}) collective-permute-start(bf16[384,1024]{1,0:T(8,128)(2,1)S(1)} %collective-permute-done.6.refs_16_), channel_id=1, source_target_pairs={{0,1},{1,0},{2,3},{3,2},{4,5},{5,4},{6,7},{7,6},{8,9},{9,8},{10,11... | collective-permute-start | bytes 2359304 | tf_op jit(solution)/shard_map/ppermute | solution.py:250
  93.9 2.3 %collective-permute-start.17 = (bf16[384,1024]{1,0:T(8,128)(2,1)S(1)}, bf16[384,1024]{1,0:T(8,128)(2,1)S(1)}, u32[]{:S(2)}, u32[]{:S(2)}) collective-permute-start(bf16[384,1024]{1,0:T(8,128)(2,1)S(1)} %collective-permute-done.9.refs_12_), channel_id=1, source_target_pairs={{0,8},{8,0},{1,9},{9,1},{2,10},{10,2},{3,11},{11,3},{4,12},{12,4},... | collective-permute-start | bytes 2359304 | tf_op jit(solution)/shard_map/ppermute | solution.py:250
  93.9 3.6 %collective-permute-start.15 = (bf16[384,1024]{1,0:T(8,128)(2,1)S(1)}, bf16[384,1024]{1,0:T(8,128)(2,1)S(1)}, u32[]{:S(2)}, u32[]{:S(2)}) collective-permute-start(bf16[384,1024]{1,0:T(8,128)(2,1)S(1)} %collective-permute-done.11.refs_8_), channel_id=1, source_target_pairs={{0,8},{8,0},{1,9},{9,1},{2,10},{10,2},{3,11},{11,3},{4,12},{12,4},... | collective-permute-start | bytes 2359304 | tf_op jit(solution)/shard_map/ppermute | solution.py:250
  94.4 4.0 %collective-permute-start.16 = (bf16[384,1024]{1,0:T(8,128)(2,1)S(1)}, bf16[384,1024]{1,0:T(8,128)(2,1)S(1)}, u32[]{:S(2)}, u32[]{:S(2)}) collective-permute-start(bf16[384,1024]{1,0:T(8,128)(2,1)S(1)} %collective-permute-done.12.refs_10_), channel_id=1, source_target_pairs={{0,8},{8,0},{1,9},{9,1},{2,10},{10,2},{3,11},{11,3},{4,12},{12,4},... | collective-permute-start | bytes 2359304 | tf_op jit(solution)/shard_map/ppermute | solution.py:250
  94.4 12.6 %collective-permute-start.19 = (bf16[384,1024]{1,0:T(8,128)(2,1)S(1)}, bf16[384,1024]{1,0:T(8,128)(2,1)S(1)}, u32[]{:S(2)}, u32[]{:S(2)}) collective-permute-start(bf16[384,1024]{1,0:T(8,128)(2,1)S(1)} %maximum_convert_fusion.refs_8_), channel_id=1, source_target_pairs={{2,4},{3,5},{4,2},{5,3},{10,12},{11,13},{12,10},{13,11},{18,20},{1... | collective-permute-start | bytes 2359304 | tf_op jit(solution)/shard_map/ppermute | solution.py:250
  95.1 20.0 %collective-permute-start.18 = (bf16[384,1024]{1,0:T(8,128)(2,1)S(1)}, bf16[384,1024]{1,0:T(8,128)(2,1)S(1)}, u32[]{:S(2)}, u32[]{:S(2)}) collective-permute-start(bf16[384,1024]{1,0:T(8,128)(2,1)S(1)} %collective-permute-done.9.refs_12_), channel_id=1, source_target_pairs={{0,1},{1,0},{2,3},{3,2},{4,5},{5,4},{6,7},{7,6},{8,9},{9,8},{10,11... | collective-permute-start | bytes 2359304 | tf_op jit(solution)/shard_map/ppermute | solution.py:250
  96.2 21.6 %collective-permute-start.14 = (bf16[384,1024]{1,0:T(8,128)(2,1)S(1)}, bf16[384,1024]{1,0:T(8,128)(2,1)S(1)}, u32[]{:S(2)}, u32[]{:S(2)}) collective-permute-start(bf16[384,1024]{1,0:T(8,128)(2,1)S(1)} %collective-permute-done.9.refs_12_), channel_id=1, source_target_pairs={{2,0},{3,1},{4,6},{5,7},{10,8},{11,9},{12,14},{13,15},{18,16},{19,... | collective-permute-start | bytes 2359304 | tf_op jit(solution)/shard_map/ppermute | solution.py:250
  117.8 5.6 %collective-permute-start.22 = (bf16[384,1024]{1,0:T(8,128)(2,1)S(1)}, bf16[384,1024]{1,0:T(8,128)(2,1)S(1)}, u32[]{:S(2)}, u32[]{:S(2)}) collective-permute-start(bf16[384,1024]{1,0:T(8,128)(2,1)S(1)} %add.209.refs_10_), channel_id=1, source_target_pairs={{0,8},{8,0},{1,9},{9,1},{2,10},{10,2},{3,11},{11,3},{4,12},{12,4},... | collective-permute-start | bytes 2359304 | tf_op jit(solution)/shard_map/ppermute | solution.py:250
  117.8 5.6 %collective-permute-start.21 = (bf16[384,1024]{1,0:T(8,128)(2,1)S(1)}, bf16[384,1024]{1,0:T(8,128)(2,1)S(1)}, u32[]{:S(2)}, u32[]{:S(2)}) collective-permute-start(bf16[384,1024]{1,0:T(8,128)(2,1)S(1)} %collective-permute-done.18.refs_8_), channel_id=1, source_target_pairs={{0,8},{8,0},{1,9},{9,1},{2,10},{10,2},{3,11},{11,3},{4,12},{12,4},... | collective-permute-start | bytes 2359304 | tf_op jit(solution)/shard_map/ppermute | solution.py:250
  118.3 19.4 %collective-permute-start.23 = (bf16[384,1024]{1,0:T(8,128)(2,1)S(1)}, bf16[384,1024]{1,0:T(8,128)(2,1)S(1)}, u32[]{:S(2)}, u32[]{:S(2)}) collective-permute-start(bf16[384,1024]{1,0:T(8,128)(2,1)S(1)} %add.209.refs_10_), channel_id=1, source_target_pairs={{0,1},{1,0},{2,3},{3,2},{4,5},{5,4},{6,7},{7,6},{8,9},{9,8},{10,11... | collective-permute-start | bytes 2359304 | tf_op jit(solution)/shard_map/ppermute | solution.py:250
  119.8 18.0 %collective-permute-start.20 = (bf16[384,1024]{1,0:T(8,128)(2,1)S(1)}, bf16[384,1024]{1,0:T(8,128)(2,1)S(1)}, u32[]{:S(2)}, u32[]{:S(2)}) collective-permute-start(bf16[384,1024]{1,0:T(8,128)(2,1)S(1)} %maximum_convert_fusion.1.refs_10_), channel_id=1, source_target_pairs={{2,4},{3,5},{4,2},{5,3},{10,12},{11,13},{12,10},{13,11},{18,20},{1... | collective-permute-start | bytes 2359304 | tf_op jit(solution)/shard_map/ppermute | solution.py:250
  120.7 19.9 %collective-permute-start.24 = (bf16[384,1024]{1,0:T(8,128)(2,1)S(1)}, bf16[384,1024]{1,0:T(8,128)(2,1)S(1)}, u32[]{:S(2)}, u32[]{:S(2)}) collective-permute-start(bf16[384,1024]{1,0:T(8,128)(2,1)S(1)} %maximum_convert_fusion.1.refs_10_), channel_id=1, source_target_pairs={{0,2},{1,3},{2,0},{3,1},{4,6},{5,7},{6,4},{7,5},{8,10},{9,11},{10,... | collective-permute-start | bytes 2359304 | tf_op jit(solution)/shard_map/ppermute | solution.py:250
  140.8 3.3 %collective-permute-start.27 = (bf16[384,1024]{1,0:T(8,128)(2,1)S(1)}, bf16[384,1024]{1,0:T(8,128)(2,1)S(1)}, u32[]{:S(2)}, u32[]{:S(2)}) collective-permute-start(bf16[384,1024]{1,0:T(8,128)(2,1)S(1)} %add.208.refs_10_), channel_id=1, source_target_pairs={{0,8},{8,0},{1,9},{9,1},{2,10},{10,2},{3,11},{11,3},{4,12},{12,4},... | collective-permute-start | bytes 2359304 | tf_op jit(solution)/shard_map/ppermute | solution.py:250
  140.9 3.4 %collective-permute-start.26 = (bf16[384,1024]{1,0:T(8,128)(2,1)S(1)}, bf16[384,1024]{1,0:T(8,128)(2,1)S(1)}, u32[]{:S(2)}, u32[]{:S(2)}) collective-permute-start(bf16[384,1024]{1,0:T(8,128)(2,1)S(1)} %collective-permute-done.23.refs_8_), channel_id=1, source_target_pairs={{0,8},{8,0},{1,9},{9,1},{2,10},{10,2},{3,11},{11,3},{4,12},{12,4},... | collective-permute-start | bytes 2359304 | tf_op jit(solution)/shard_map/ppermute | solution.py:250
  141.4 4.0 %collective-permute-start.28 = (bf16[384,1024]{1,0:T(8,128)(2,1)S(1)}, bf16[384,1024]{1,0:T(8,128)(2,1)S(1)}, u32[]{:S(2)}, u32[]{:S(2)}) collective-permute-start(bf16[384,1024]{1,0:T(8,128)(2,1)S(1)} %collective-permute-done.24.refs_12_), channel_id=1, source_target_pairs={{0,8},{8,0},{1,9},{9,1},{2,10},{10,2},{3,11},{11,3},{4,12},{12,4},... | collective-permute-start | bytes 2359304 | tf_op jit(solution)/shard_map/ppermute | solution.py:250
  141.5 19.9 %collective-permute-start.25 = (bf16[384,1024]{1,0:T(8,128)(2,1)S(1)}, bf16[384,1024]{1,0:T(8,128)(2,1)S(1)}, u32[]{:S(2)}, u32[]{:S(2)}) collective-permute-start(bf16[384,1024]{1,0:T(8,128)(2,1)S(1)} %add.208.refs_10_), channel_id=1, source_target_pairs={{0,1},{1,0},{2,3},{3,2},{4,5},{5,4},{6,7},{7,6},{8,9},{9,8},{10,11... | collective-permute-start | bytes 2359304 | tf_op jit(solution)/shard_map/ppermute | solution.py:250
  142.4 19.6 %collective-permute-start.30 = (bf16[384,1024]{1,0:T(8,128)(2,1)S(1)}, bf16[384,1024]{1,0:T(8,128)(2,1)S(1)}, u32[]{:S(2)}, u32[]{:S(2)}) collective-permute-start(bf16[384,1024]{1,0:T(8,128)(2,1)S(1)} %collective-permute-done.4.refs_14_), channel_id=1, source_target_pairs={{0,2},{1,3},{2,0},{3,1},{4,6},{5,7},{6,4},{7,5},{8,10},{9,11},{10,... | collective-permute-start | bytes 2359304 | tf_op jit(solution)/shard_map/ppermute | solution.py:250
  161.4 2.3 %collective-permute-start.29 = (bf16[384,1024]{1,0:T(8,128)(2,1)S(1)}, bf16[384,1024]{1,0:T(8,128)(2,1)S(1)}, u32[]{:S(2)}, u32[]{:S(2)}) collective-permute-start(bf16[384,1024]{1,0:T(8,128)(2,1)S(1)} %collective-permute-done.25.refs_8_), channel_id=1, source_target_pairs={{0,8},{8,0},{1,9},{9,1},{2,10},{10,2},{3,11},{11,3},{4,12},{12,4},... | collective-permute-start | bytes 2359304 | tf_op jit(solution)/shard_map/ppermute | solution.py:250
  162.0 2.8 %collective-permute-start.31 = (bf16[384,1024]{1,0:T(8,128)(2,1)S(1)}, bf16[384,1024]{1,0:T(8,128)(2,1)S(1)}, u32[]{:S(2)}, u32[]{:S(2)}) collective-permute-start(bf16[384,1024]{1,0:T(8,128)(2,1)S(1)} %collective-permute-done.30.refs_10_), channel_id=1, source_target_pairs={{0,8},{8,0},{1,9},{9,1},{2,10},{10,2},{3,11},{11,3},{4,12},{12,4},... | collective-permute-start | bytes 2359304 | tf_op jit(solution)/shard_map/ppermute | solution.py:250
  (6 other events, 27.2 us)

commit v4 on v3

--- a/solution.py
+++ b/solution.py
@@ -324,7 +324,7 @@
     m.keep(p300=n3a)
     state = work(2, state)
 
-    m.after(x3a, gb, n1b)
+    m.after(x3a, gb)
     n3b = fb + gb
     x3b = m.send(n3b, ACROSS, early=1)
     x1b = m.send(x0b, NEXT)

time: 174 us -> 174 us (level)
  no operation moved by 1% of the time
where the time goes in v4:
time: 174 us; the launch traced here: 173 us
  waiting for transfers between devices  90.6 us (52%)
  Pallas kernels  44.3 us (25%)
  starting transfers between devices  24.9 us (14%)
  matrix products  8.56 us (5%)
  other arithmetic  4.37 us (3%)
    ppermute x29, waiting for transfers between devices, send(): return lax.ppermute(array, axis, pairs)  90.6 us
    pallas_call x5, Pallas kernels, tiles(): pl.pallas_call(functools.partial(tiles_kernel, tuple(sources), len(pieces...  44.3 us
    ppermute x29, starting transfers between devices, send(): return lax.ppermute(array, axis, pairs)  23.7 us
    dot_general x1, matrix products, encode(): near[order[0]] = dot(mine, enc_weight[:, halves[order[0]]])  3.81 us
  transfers between devices with their start and end apart: 32, of which 17 were waited for; matrix products, arithmetic and copies ran while one was open for 5% of the time, Pallas kernels for 21%

profile of v4, /device:TPU:0, one launch (start us, length us, event | category | flops | bytes accessed | tf_op | source)
XLA Modules:
  0.0 173.3 jit_solution(10151580043749818161)
XLA Ops:
  0.0 2.1 %broadcast_select_fusion = (bf16[384,1792]{1,0:T(8,128)(2,1)S(1)}, bf16[384,1792]{1,0:T(8,128)(2,1)S(1)}) fusion(pred[]{:T(512)S(6)} %eq.252, bf16[384,3584]{1,0:T(8,128)(2,1)} %bitcast.22), kind=kLoop, calls=%fused_computation.13 | loop fusion | flops 1376256 | bytes 5505025 | tf_op jit(solution)/shard_map/jit(_where)/select_n | solution.py:347
  2.6 3.8 %fusion.6 = f32[384,1024]{1,0:T(8,128)S(1)} fusion(bf16[384,1792]{1,0:T(8,128)(2,1)S(1)} %get-tuple-element.47, bf16[1792,2048]{1,0:T(8,128)(2,1)} %param.7), kind=kOutput, calls=%fused_computation.6 | convolution fusion | flops 1409286144 | bytes 6619136 | tf_op jit(solution)/shard_map/dot_general | solution.py:354
  6.5 1.6 fusion.8
  8.2 1.6 fusion.11
  10.3 1.6 fusion
  12.6 4.0 %collective-permute-start.6 = (bf16[384,1024]{1,0:T(8,128)(2,1)S(1)}, bf16[384,1024]{1,0:T(8,128)(2,1)S(1)}, u32[]{:S(2)}, u32[]{:S(2)}) collective-permute-start(bf16[384,1024]{1,0:T(8,128)(2,1)S(1)} %maximum_convert_fusion.refs_8_), channel_id=1, source_target_pairs={{0,4},{1,5},{4,0},{5,1},{2,6},{3,7},{6,2},{7,3},{8,12},{9,13},{12,... | collective-permute-start | bytes 2359304 | tf_op jit(solution)/shard_map/ppermute | solution.py:250
  17.0 1.5 collective-permute-start.3
  18.5 1.6 collective-permute-start.5
  20.9 30.5 %collective-permute-done.6.refs_16_ = bf16[384,1024]{1,0:T(8,128)(2,1)S(1)} collective-permute-done((bf16[384,1024]{1,0:T(8,128)(2,1)S(1)}, bf16[384,1024]{1,0:T(8,128)(2,1)S(1)}, u32[]{:S(2)}, u32[]{:S(2)}) %collective-permute-start.6) | collective-permute-done | bytes 786464 | tf_op jit(solution)/shard_map/ppermute | solution.py:250
  51.6 1.7 collective-permute-done.5.refs_15_
  54.3 1.3 collective-permute-start.11
  55.6 1.3 collective-permute-start.13
  57.7 1.7 collective-permute-done.10.refs_13_
  59.4 8.2 %shard_map.64 = (bf16[67,256,512]{2,1,0:T(8,128)(2,1)}, bf16[32,2,384,512]{3,2,1,0:T(8,128)(2,1)}, s32[1]{0:T(128)}) custom-call(s32[16]{0:T(128)S(1)} %stack.67.refs_0_, s32[67]{0:T(128)S(1)} %select_reduce_fusion.2.refs_1_, s32[8]{0:T(128)S(1)} %convert_reduce_fusion.1.refs_2_, s32[67]{0:T(128)S(1)} %get-tuple-element.88.refs_3_, ...), custom_call_target="tpu_custom_call" | custom-call | flops 1000 | bytes 1000 | tf_op jit(solution)/shard_map/pallas_call | solution.py:176
  67.6 24.0 %collective-permute-done.9.refs_12_ = bf16[384,1024]{1,0:T(8,128)(2,1)S(1)} collective-permute-done((bf16[384,1024]{1,0:T(8,128)(2,1)S(1)}, bf16[384,1024]{1,0:T(8,128)(2,1)S(1)}, u32[]{:S(2)}, u32[]{:S(2)}) %collective-permute-start.9) | collective-permute-done | bytes 786464 | tf_op jit(solution)/shard_map/ppermute | solution.py:250
  91.6 2.3 %collective-permute-done.13 = bf16[384,1024]{1,0:T(8,128)(2,1)S(1)} collective-permute-done((bf16[384,1024]{1,0:T(8,128)(2,1)S(1)}, bf16[384,1024]{1,0:T(8,128)(2,1)S(1)}, u32[]{:S(2)}, u32[]{:S(2)}) %collective-permute-start.13) | collective-permute-done | bytes 786464 | tf_op jit(solution)/shard_map/ppermute | solution.py:250
  96.2 1.3 collective-permute-start.14
  98.4 9.6 %shard_map.65 = (bf16[67,256,512]{2,1,0:T(8,128)(2,1)}, bf16[32,2,384,512]{3,2,1,0:T(8,128)(2,1)}, s32[1]{0:T(128)}) custom-call(s32[16]{0:T(128)S(1)} %stack.67.refs_0_, s32[67]{0:T(128)S(1)} %select_reduce_fusion.2.refs_1_, s32[8]{0:T(128)S(1)} %convert_reduce_fusion.1.refs_2_, ...), custom_call_target="tpu_custom_call", output_to_operand_aliasing={{0}: (14, {}), {1}: (15, {})} | custom-call | flops 1000 | bytes 1000 | tf_op jit(solution)/shard_map/pallas_call | solution.py:176
  108.4 6.8 %collective-permute-done.18.refs_8_ = bf16[384,1024]{1,0:T(8,128)(2,1)S(1)} collective-permute-done((bf16[384,1024]{1,0:T(8,128)(2,1)S(1)}, bf16[384,1024]{1,0:T(8,128)(2,1)S(1)}, u32[]{:S(2)}, u32[]{:S(2)}) %collective-permute-start.18) | collective-permute-done | bytes 786464 | tf_op jit(solution)/shard_map/ppermute | solution.py:250
  115.1 2.6 %collective-permute-done.14 = bf16[384,1024]{1,0:T(8,128)(2,1)S(1)} collective-permute-done((bf16[384,1024]{1,0:T(8,128)(2,1)S(1)}, bf16[384,1024]{1,0:T(8,128)(2,1)S(1)}, u32[]{:S(2)}, u32[]{:S(2)}) %collective-permute-start.14) | collective-permute-done | bytes 786464 | tf_op jit(solution)/shard_map/ppermute | solution.py:250
  118.3 1.5 collective-permute-start.23
  120.7 2.7 %collective-permute-start.27 = (bf16[384,1024]{1,0:T(8,128)(2,1)S(1)}, bf16[384,1024]{1,0:T(8,128)(2,1)S(1)}, u32[]{:S(2)}, u32[]{:S(2)}) collective-permute-start(bf16[384,1024]{1,0:T(8,128)(2,1)S(1)} %maximum_convert_fusion.1.refs_10_), channel_id=1, source_target_pairs={{0,2},{1,3},{2,0},{3,1},{4,6},{5,7},{6,4},{7,5},{8,10},{9,11},{10,... | collective-permute-start | bytes 2359304 | tf_op jit(solution)/shard_map/ppermute | solution.py:250
  123.4 7.6 %shard_map.66 = (bf16[67,256,512]{2,1,0:T(8,128)(2,1)}, bf16[32,2,384,512]{3,2,1,0:T(8,128)(2,1)}, s32[1]{0:T(128)}) custom-call(s32[16]{0:T(128)S(1)} %stack.67.refs_0_, s32[67]{0:T(128)S(1)} %select_reduce_fusion.2.refs_1_, s32[8]{0:T(128)S(1)} %convert_reduce_fusion.1.refs_2_, ...), custom_call_target="tpu_custom_call", output_to_operand_aliasing={{0}: (12, {}), {1}: (13, {})} | custom-call | flops 1000 | bytes 1000 | tf_op jit(solution)/shard_map/pallas_call | solution.py:176
  131.0 6.7 %collective-permute-done.23.refs_8_ = bf16[384,1024]{1,0:T(8,128)(2,1)S(1)} collective-permute-done((bf16[384,1024]{1,0:T(8,128)(2,1)S(1)}, bf16[384,1024]{1,0:T(8,128)(2,1)S(1)}, u32[]{:S(2)}, u32[]{:S(2)}) %collective-permute-start.23) | collective-permute-done | bytes 786464 | tf_op jit(solution)/shard_map/ppermute | solution.py:250
  137.7 2.8 %collective-permute-done.27.refs_12_ = bf16[384,1024]{1,0:T(8,128)(2,1)S(1)} collective-permute-done((bf16[384,1024]{1,0:T(8,128)(2,1)S(1)}, bf16[384,1024]{1,0:T(8,128)(2,1)S(1)}, u32[]{:S(2)}, u32[]{:S(2)}) %collective-permute-start.27) | collective-permute-done | bytes 786464 | tf_op jit(solution)/shard_map/ppermute | solution.py:250
  142.4 1.7 %collective-permute-start.30 = (bf16[384,1024]{1,0:T(8,128)(2,1)S(1)}, bf16[384,1024]{1,0:T(8,128)(2,1)S(1)}, u32[]{:S(2)}, u32[]{:S(2)}) collective-permute-start(bf16[384,1024]{1,0:T(8,128)(2,1)S(1)} %collective-permute-done.4.refs_14_), channel_id=1, source_target_pairs={{0,2},{1,3},{2,0},{3,1},{4,6},{5,7},{6,4},{7,5},{8,10},{9,11},{10,... | collective-permute-start | bytes 2359304 | tf_op jit(solution)/shard_map/ppermute | solution.py:250
  144.3 1.1 collective-permute-done.28.refs_13_
  145.4 10.5 %shard_map.67 = (bf16[67,256,512]{2,1,0:T(8,128)(2,1)}, bf16[32,2,384,512]{3,2,1,0:T(8,128)(2,1)}, s32[1]{0:T(128)}) custom-call(s32[16]{0:T(128)S(1)} %stack.67.refs_0_, s32[67]{0:T(128)S(1)} %select_reduce_fusion.2.refs_1_, s32[8]{0:T(128)S(1)} %convert_reduce_fusion.1.refs_2_, ...), custom_call_target="tpu_custom_call", output_to_operand_aliasing={{0}: (14, {}), {1}: (15, {})} | custom-call | flops 1000 | bytes 1000 | tf_op jit(solution)/shard_map/pallas_call | solution.py:176
  155.9 5.5 %collective-permute-done.24.refs_8_ = bf16[384,1024]{1,0:T(8,128)(2,1)S(1)} collective-permute-done((bf16[384,1024]{1,0:T(8,128)(2,1)S(1)}, bf16[384,1024]{1,0:T(8,128)(2,1)S(1)}, u32[]{:S(2)}, u32[]{:S(2)}) %collective-permute-start.24) | collective-permute-done | bytes 786464 | tf_op jit(solution)/shard_map/ppermute | solution.py:250
  162.0 1.7 collective-permute-done.29.refs_9_
  163.7 1.1 collective-permute-done.31.refs_11_
  164.8 8.4 %shard_map.68 = (bf16[67,256,512]{2,1,0:T(8,128)(2,1)}, bf16[32,2,384,512]{3,2,1,0:T(8,128)(2,1)}, s32[1]{0:T(128)}) custom-call(s32[16]{0:T(128)S(1)} %stack.67.refs_0_, s32[67]{0:T(128)S(1)} %select_reduce_fusion.2.refs_1_, s32[8]{0:T(128)S(1)} %convert_reduce_fusion.1.refs_2_, ...), custom_call_target="tpu_custom_call", output_to_operand_aliasing={{0}: (12, {}), {1}: (13, {})} | custom-call | flops 1000 | bytes 1000 | tf_op jit(solution)/shard_map/pallas_call | solution.py:176
  (70 shorter events, 12.7 us)
Async XLA Ops:
  2.1 4.3 %collective-permute-start = (bf16[384,1792]{1,0:T(8,128)(2,1)S(1)}, bf16[384,1792]{1,0:T(8,128)(2,1)S(1)}, u32[]{:S(2)}, u32[]{:S(2)}) collective-permute-start(bf16[384,1792]{1,0:T(8,128)(2,1)S(1)} %get-tuple-element.91), channel_id=1, source_target_pairs={{0,8},{8,0},{1,9},{9,1},{2,10},{10,2},{3,11},{11,3},{4,12},{12,4},... | collective-permute-start | bytes 4128776 | tf_op jit(solution)/shard_map/ppermute | solution.py:348
  8.1 3.8 %collective-permute-start.1 = (bf16[384,1024]{1,0:T(8,128)(2,1)S(1)}, bf16[384,1024]{1,0:T(8,128)(2,1)S(1)}, u32[]{:S(2)}, u32[]{:S(2)}) collective-permute-start(bf16[384,1024]{1,0:T(8,128)(2,1)S(1)} %fusion.8), channel_id=1, source_target_pairs={{0,8},{8,0},{1,9},{9,1},{2,10},{10,2},{3,11},{11,3},{4,12},{12,4},... | collective-permute-start | bytes 2359304 | tf_op jit(solution)/shard_map/ppermute | solution.py:360
  9.8 2.5 %collective-permute-start.2 = (bf16[384,1024]{1,0:T(8,128)(2,1)S(1)}, bf16[384,1024]{1,0:T(8,128)(2,1)S(1)}, u32[]{:S(2)}, u32[]{:S(2)}) collective-permute-start(bf16[384,1024]{1,0:T(8,128)(2,1)S(1)} %fusion.11), channel_id=1, source_target_pairs={{0,8},{8,0},{1,9},{9,1},{2,10},{10,2},{3,11},{11,3},{4,12},{12,4},... | collective-permute-start | bytes 2359304 | tf_op jit(solution)/shard_map/ppermute | solution.py:360
  12.6 38.8 %collective-permute-start.6 = (bf16[384,1024]{1,0:T(8,128)(2,1)S(1)}, bf16[384,1024]{1,0:T(8,128)(2,1)S(1)}, u32[]{:S(2)}, u32[]{:S(2)}) collective-permute-start(bf16[384,1024]{1,0:T(8,128)(2,1)S(1)} %maximum_convert_fusion.refs_8_), channel_id=1, source_target_pairs={{0,4},{1,5},{4,0},{5,1},{2,6},{3,7},{6,2},{7,3},{8,12},{9,13},{12,... | collective-permute-start | bytes 2359304 | tf_op jit(solution)/shard_map/ppermute | solution.py:250
  17.0 34.6 %collective-permute-start.3 = (bf16[384,1024]{1,0:T(8,128)(2,1)S(1)}, bf16[384,1024]{1,0:T(8,128)(2,1)S(1)}, u32[]{:S(2)}, u32[]{:S(2)}) collective-permute-start(bf16[384,1024]{1,0:T(8,128)(2,1)S(1)} %maximum_convert_fusion.refs_8_), channel_id=1, source_target_pairs={{0,1},{1,0},{2,3},{3,2},{4,5},{5,4},{6,7},{7,6},{8,9},{9,8},{10,11... | collective-permute-start | bytes 2359304 | tf_op jit(solution)/shard_map/ppermute | solution.py:250
  18.5 34.8 %collective-permute-start.5 = (bf16[384,1024]{1,0:T(8,128)(2,1)S(1)}, bf16[384,1024]{1,0:T(8,128)(2,1)S(1)}, u32[]{:S(2)}, u32[]{:S(2)}) collective-permute-start(bf16[384,1024]{1,0:T(8,128)(2,1)S(1)} %maximum_convert_fusion.refs_8_), channel_id=1, source_target_pairs={{0,2},{1,3},{2,0},{3,1},{4,6},{5,7},{6,4},{7,5},{8,10},{9,11},{10,... | collective-permute-start | bytes 2359304 | tf_op jit(solution)/shard_map/ppermute | solution.py:250
  20.1 33.2 %collective-permute-start.4 = (bf16[384,1024]{1,0:T(8,128)(2,1)S(1)}, bf16[384,1024]{1,0:T(8,128)(2,1)S(1)}, u32[]{:S(2)}, u32[]{:S(2)}) collective-permute-start(bf16[384,1024]{1,0:T(8,128)(2,1)S(1)} %maximum_convert_fusion.1.refs_10_), channel_id=1, source_target_pairs={{0,1},{1,0},{2,3},{3,2},{4,5},{5,4},{6,7},{7,6},{8,9},{9,8},{10,11... | collective-permute-start | bytes 2359304 | tf_op jit(solution)/shard_map/ppermute | solution.py:250
  20.8 32.8 %collective-permute-start.7 = (bf16[384,1024]{1,0:T(8,128)(2,1)S(1)}, bf16[384,1024]{1,0:T(8,128)(2,1)S(1)}, u32[]{:S(2)}, u32[]{:S(2)}) collective-permute-start(bf16[384,1024]{1,0:T(8,128)(2,1)S(1)} %maximum_convert_fusion.refs_8_), channel_id=1, source_target_pairs={{0,8},{8,0},{1,9},{9,1},{2,10},{10,2},{3,11},{11,3},{4,12},{12,4},... | collective-permute-start | bytes 2359304 | tf_op jit(solution)/shard_map/ppermute | solution.py:250
  51.4 2.3 %collective-permute-start.8 = (bf16[384,1024]{1,0:T(8,128)(2,1)S(1)}, bf16[384,1024]{1,0:T(8,128)(2,1)S(1)}, u32[]{:S(2)}, u32[]{:S(2)}) collective-permute-start(bf16[384,1024]{1,0:T(8,128)(2,1)S(1)} %maximum_convert_fusion.1.refs_10_), channel_id=1, source_target_pairs={{0,8},{8,0},{1,9},{9,1},{2,10},{10,2},{3,11},{11,3},{4,12},{12,4},... | collective-permute-start | bytes 2359304 | tf_op jit(solution)/shard_map/ppermute | solution.py:250
  53.7 5.7 %collective-permute-start.10 = (bf16[1536,1024]{1,0:T(8,128)(2,1)S(1)}, bf16[1536,1024]{1,0:T(8,128)(2,1)S(1)}, u32[]{:S(2)}, u32[]{:S(2)}) collective-permute-start(bf16[1536,1024]{1,0:T(8,128)(2,1)S(1)} %pad_maximum_fusion), channel_id=1, source_target_pairs={{0,8},{8,0},{1,9},{9,1},{2,10},{10,2},{3,11},{11,3},{4,12},{12,4},... | collective-permute-start | bytes 9437192 | tf_op jit(solution)/shard_map/ppermute | solution.py:250
  53.8 37.8 %collective-permute-start.9 = (bf16[384,1024]{1,0:T(8,128)(2,1)S(1)}, bf16[384,1024]{1,0:T(8,128)(2,1)S(1)}, u32[]{:S(2)}, u32[]{:S(2)}) collective-permute-start(bf16[384,1024]{1,0:T(8,128)(2,1)S(1)} %maximum_convert_fusion.1.refs_10_), channel_id=1, source_target_pairs={{0,4},{1,5},{4,0},{5,1},{2,6},{3,7},{6,2},{7,3},{8,12},{9,13},{12,... | collective-permute-start | bytes 2359304 | tf_op jit(solution)/shard_map/ppermute | solution.py:250
  54.3 37.2 %collective-permute-start.11 = (bf16[384,1024]{1,0:T(8,128)(2,1)S(1)}, bf16[384,1024]{1,0:T(8,128)(2,1)S(1)}, u32[]{:S(2)}, u32[]{:S(2)}) collective-permute-start(bf16[384,1024]{1,0:T(8,128)(2,1)S(1)} %collective-permute-done.5.refs_15_), channel_id=1, source_target_pairs={{0,1},{1,0},{2,3},{3,2},{4,5},{5,4},{6,7},{7,6},{8,9},{9,8},{10,11... | collective-permute-start | bytes 2359304 | tf_op jit(solution)/shard_map/ppermute | solution.py:250
  55.6 38.3 %collective-permute-start.13 = (bf16[384,1024]{1,0:T(8,128)(2,1)S(1)}, bf16[384,1024]{1,0:T(8,128)(2,1)S(1)}, u32[]{:S(2)}, u32[]{:S(2)}) collective-permute-start(bf16[384,1024]{1,0:T(8,128)(2,1)S(1)} %collective-permute-done.6.refs_16_), channel_id=1, source_target_pairs={{2,0},{3,1},{4,6},{5,7},{10,8},{11,9},{12,14},{13,15},{18,16},{19,... | collective-permute-start | bytes 2359304 | tf_op jit(solution)/shard_map/ppermute | solution.py:250
  56.9 37.0 %collective-permute-start.12 = (bf16[384,1024]{1,0:T(8,128)(2,1)S(1)}, bf16[384,1024]{1,0:T(8,128)(2,1)S(1)}, u32[]{:S(2)}, u32[]{:S(2)}) collective-permute-start(bf16[384,1024]{1,0:T(8,128)(2,1)S(1)} %collective-permute-done.6.refs_16_), channel_id=1, source_target_pairs={{0,1},{1,0},{2,3},{3,2},{4,5},{5,4},{6,7},{7,6},{8,9},{9,8},{10,11... | collective-permute-start | bytes 2359304 | tf_op jit(solution)/shard_map/ppermute | solution.py:250
  93.9 2.3 %collective-permute-start.17 = (bf16[384,1024]{1,0:T(8,128)(2,1)S(1)}, bf16[384,1024]{1,0:T(8,128)(2,1)S(1)}, u32[]{:S(2)}, u32[]{:S(2)}) collective-permute-start(bf16[384,1024]{1,0:T(8,128)(2,1)S(1)} %collective-permute-done.9.refs_12_), channel_id=1, source_target_pairs={{0,8},{8,0},{1,9},{9,1},{2,10},{10,2},{3,11},{11,3},{4,12},{12,4},... | collective-permute-start | bytes 2359304 | tf_op jit(solution)/shard_map/ppermute | solution.py:250
  93.9 3.6 %collective-permute-start.15 = (bf16[384,1024]{1,0:T(8,128)(2,1)S(1)}, bf16[384,1024]{1,0:T(8,128)(2,1)S(1)}, u32[]{:S(2)}, u32[]{:S(2)}) collective-permute-start(bf16[384,1024]{1,0:T(8,128)(2,1)S(1)} %collective-permute-done.11.refs_8_), channel_id=1, source_target_pairs={{0,8},{8,0},{1,9},{9,1},{2,10},{10,2},{3,11},{11,3},{4,12},{12,4},... | collective-permute-start | bytes 2359304 | tf_op jit(solution)/shard_map/ppermute | solution.py:250
  94.4 4.0 %collective-permute-start.16 = (bf16[384,1024]{1,0:T(8,128)(2,1)S(1)}, bf16[384,1024]{1,0:T(8,128)(2,1)S(1)}, u32[]{:S(2)}, u32[]{:S(2)}) collective-permute-start(bf16[384,1024]{1,0:T(8,128)(2,1)S(1)} %collective-permute-done.12.refs_10_), channel_id=1, source_target_pairs={{0,8},{8,0},{1,9},{9,1},{2,10},{10,2},{3,11},{11,3},{4,12},{12,4},... | collective-permute-start | bytes 2359304 | tf_op jit(solution)/shard_map/ppermute | solution.py:250
  94.4 13.6 %collective-permute-start.19 = (bf16[384,1024]{1,0:T(8,128)(2,1)S(1)}, bf16[384,1024]{1,0:T(8,128)(2,1)S(1)}, u32[]{:S(2)}, u32[]{:S(2)}) collective-permute-start(bf16[384,1024]{1,0:T(8,128)(2,1)S(1)} %maximum_convert_fusion.refs_8_), channel_id=1, source_target_pairs={{2,4},{3,5},{4,2},{5,3},{10,12},{11,13},{12,10},{13,11},{18,20},{1... | collective-permute-start | bytes 2359304 | tf_op jit(solution)/shard_map/ppermute | solution.py:250
  95.1 20.0 %collective-permute-start.18 = (bf16[384,1024]{1,0:T(8,128)(2,1)S(1)}, bf16[384,1024]{1,0:T(8,128)(2,1)S(1)}, u32[]{:S(2)}, u32[]{:S(2)}) collective-permute-start(bf16[384,1024]{1,0:T(8,128)(2,1)S(1)} %collective-permute-done.9.refs_12_), channel_id=1, source_target_pairs={{0,1},{1,0},{2,3},{3,2},{4,5},{5,4},{6,7},{7,6},{8,9},{9,8},{10,11... | collective-permute-start | bytes 2359304 | tf_op jit(solution)/shard_map/ppermute | solution.py:250
  96.2 21.6 %collective-permute-start.14 = (bf16[384,1024]{1,0:T(8,128)(2,1)S(1)}, bf16[384,1024]{1,0:T(8,128)(2,1)S(1)}, u32[]{:S(2)}, u32[]{:S(2)}) collective-permute-start(bf16[384,1024]{1,0:T(8,128)(2,1)S(1)} %collective-permute-done.9.refs_12_), channel_id=1, source_target_pairs={{2,0},{3,1},{4,6},{5,7},{10,8},{11,9},{12,14},{13,15},{18,16},{19,... | collective-permute-start | bytes 2359304 | tf_op jit(solution)/shard_map/ppermute | solution.py:250
  117.8 5.6 %collective-permute-start.22 = (bf16[384,1024]{1,0:T(8,128)(2,1)S(1)}, bf16[384,1024]{1,0:T(8,128)(2,1)S(1)}, u32[]{:S(2)}, u32[]{:S(2)}) collective-permute-start(bf16[384,1024]{1,0:T(8,128)(2,1)S(1)} %add.209.refs_10_), channel_id=1, source_target_pairs={{0,8},{8,0},{1,9},{9,1},{2,10},{10,2},{3,11},{11,3},{4,12},{12,4},... | collective-permute-start | bytes 2359304 | tf_op jit(solution)/shard_map/ppermute | solution.py:250
  117.8 5.6 %collective-permute-start.21 = (bf16[384,1024]{1,0:T(8,128)(2,1)S(1)}, bf16[384,1024]{1,0:T(8,128)(2,1)S(1)}, u32[]{:S(2)}, u32[]{:S(2)}) collective-permute-start(bf16[384,1024]{1,0:T(8,128)(2,1)S(1)} %collective-permute-done.18.refs_8_), channel_id=1, source_target_pairs={{0,8},{8,0},{1,9},{9,1},{2,10},{10,2},{3,11},{11,3},{4,12},{12,4},... | collective-permute-start | bytes 2359304 | tf_op jit(solution)/shard_map/ppermute | solution.py:250
  118.3 19.4 %collective-permute-start.23 = (bf16[384,1024]{1,0:T(8,128)(2,1)S(1)}, bf16[384,1024]{1,0:T(8,128)(2,1)S(1)}, u32[]{:S(2)}, u32[]{:S(2)}) collective-permute-start(bf16[384,1024]{1,0:T(8,128)(2,1)S(1)} %add.209.refs_10_), channel_id=1, source_target_pairs={{0,1},{1,0},{2,3},{3,2},{4,5},{5,4},{6,7},{7,6},{8,9},{9,8},{10,11... | collective-permute-start | bytes 2359304 | tf_op jit(solution)/shard_map/ppermute | solution.py:250
  119.8 18.0 %collective-permute-start.20 = (bf16[384,1024]{1,0:T(8,128)(2,1)S(1)}, bf16[384,1024]{1,0:T(8,128)(2,1)S(1)}, u32[]{:S(2)}, u32[]{:S(2)}) collective-permute-start(bf16[384,1024]{1,0:T(8,128)(2,1)S(1)} %maximum_convert_fusion.1.refs_10_), channel_id=1, source_target_pairs={{2,4},{3,5},{4,2},{5,3},{10,12},{11,13},{12,10},{13,11},{18,20},{1... | collective-permute-start | bytes 2359304 | tf_op jit(solution)/shard_map/ppermute | solution.py:250
  120.7 19.9 %collective-permute-start.27 = (bf16[384,1024]{1,0:T(8,128)(2,1)S(1)}, bf16[384,1024]{1,0:T(8,128)(2,1)S(1)}, u32[]{:S(2)}, u32[]{:S(2)}) collective-permute-start(bf16[384,1024]{1,0:T(8,128)(2,1)S(1)} %maximum_convert_fusion.1.refs_10_), channel_id=1, source_target_pairs={{0,2},{1,3},{2,0},{3,1},{4,6},{5,7},{6,4},{7,5},{8,10},{9,11},{10,... | collective-permute-start | bytes 2359304 | tf_op jit(solution)/shard_map/ppermute | solution.py:250
  140.8 3.3 %collective-permute-start.26 = (bf16[384,1024]{1,0:T(8,128)(2,1)S(1)}, bf16[384,1024]{1,0:T(8,128)(2,1)S(1)}, u32[]{:S(2)}, u32[]{:S(2)}) collective-permute-start(bf16[384,1024]{1,0:T(8,128)(2,1)S(1)} %add.208.refs_10_), channel_id=1, source_target_pairs={{0,8},{8,0},{1,9},{9,1},{2,10},{10,2},{3,11},{11,3},{4,12},{12,4},... | collective-permute-start | bytes 2359304 | tf_op jit(solution)/shard_map/ppermute | solution.py:250
  140.9 3.4 %collective-permute-start.25 = (bf16[384,1024]{1,0:T(8,128)(2,1)S(1)}, bf16[384,1024]{1,0:T(8,128)(2,1)S(1)}, u32[]{:S(2)}, u32[]{:S(2)}) collective-permute-start(bf16[384,1024]{1,0:T(8,128)(2,1)S(1)} %collective-permute-done.23.refs_8_), channel_id=1, source_target_pairs={{0,8},{8,0},{1,9},{9,1},{2,10},{10,2},{3,11},{11,3},{4,12},{12,4},... | collective-permute-start | bytes 2359304 | tf_op jit(solution)/shard_map/ppermute | solution.py:250
  141.4 4.0 %collective-permute-start.28 = (bf16[384,1024]{1,0:T(8,128)(2,1)S(1)}, bf16[384,1024]{1,0:T(8,128)(2,1)S(1)}, u32[]{:S(2)}, u32[]{:S(2)}) collective-permute-start(bf16[384,1024]{1,0:T(8,128)(2,1)S(1)} %collective-permute-done.27.refs_12_), channel_id=1, source_target_pairs={{0,8},{8,0},{1,9},{9,1},{2,10},{10,2},{3,11},{11,3},{4,12},{12,4},... | collective-permute-start | bytes 2359304 | tf_op jit(solution)/shard_map/ppermute | solution.py:250
  141.5 19.9 %collective-permute-start.24 = (bf16[384,1024]{1,0:T(8,128)(2,1)S(1)}, bf16[384,1024]{1,0:T(8,128)(2,1)S(1)}, u32[]{:S(2)}, u32[]{:S(2)}) collective-permute-start(bf16[384,1024]{1,0:T(8,128)(2,1)S(1)} %add.208.refs_10_), channel_id=1, source_target_pairs={{0,1},{1,0},{2,3},{3,2},{4,5},{5,4},{6,7},{7,6},{8,9},{9,8},{10,11... | collective-permute-start | bytes 2359304 | tf_op jit(solution)/shard_map/ppermute | solution.py:250
  142.4 19.6 %collective-permute-start.30 = (bf16[384,1024]{1,0:T(8,128)(2,1)S(1)}, bf16[384,1024]{1,0:T(8,128)(2,1)S(1)}, u32[]{:S(2)}, u32[]{:S(2)}) collective-permute-start(bf16[384,1024]{1,0:T(8,128)(2,1)S(1)} %collective-permute-done.4.refs_14_), channel_id=1, source_target_pairs={{0,2},{1,3},{2,0},{3,1},{4,6},{5,7},{6,4},{7,5},{8,10},{9,11},{10,... | collective-permute-start | bytes 2359304 | tf_op jit(solution)/shard_map/ppermute | solution.py:250
  161.4 2.3 %collective-permute-start.29 = (bf16[384,1024]{1,0:T(8,128)(2,1)S(1)}, bf16[384,1024]{1,0:T(8,128)(2,1)S(1)}, u32[]{:S(2)}, u32[]{:S(2)}) collective-permute-start(bf16[384,1024]{1,0:T(8,128)(2,1)S(1)} %collective-permute-done.24.refs_8_), channel_id=1, source_target_pairs={{0,8},{8,0},{1,9},{9,1},{2,10},{10,2},{3,11},{11,3},{4,12},{12,4},... | collective-permute-start | bytes 2359304 | tf_op jit(solution)/shard_map/ppermute | solution.py:250
  162.0 2.8 %collective-permute-start.31 = (bf16[384,1024]{1,0:T(8,128)(2,1)S(1)}, bf16[384,1024]{1,0:T(8,128)(2,1)S(1)}, u32[]{:S(2)}, u32[]{:S(2)}) collective-permute-start(bf16[384,1024]{1,0:T(8,128)(2,1)S(1)} %collective-permute-done.30.refs_10_), channel_id=1, source_target_pairs={{0,8},{8,0},{1,9},{9,1},{2,10},{10,2},{3,11},{11,3},{4,12},{12,4},... | collective-permute-start | bytes 2359304 | tf_op jit(solution)/shard_map/ppermute | solution.py:250
  (6 other events, 27.2 us)
